TPU v7x, 256 devices: a whole 4x4x8 slice. The times are simulated.
256 devices in a mesh: dm: 4 (over x), fft: 64 (over y, z, core).
Axes of the slice: x: 4, y: 4, z: 8, core: 2. Of those that a mesh axis runs over, the one named last changes fastest.
Arguments:
- series: float32 [16777216], P(('dm', 'fft')), parts along dimension 0, may hold values from -6 to 6
- filters: float32 [32, 16], replicated, may hold values from -1.5 to 1.5
- delays: int32 [2, 1024], P(None, 'fft'), may hold values from -48 to 48, as said below
- phases: int32 [2, 1024], P(None, 'fft'), may hold values from 0 to 31
Outputs:
- harmonic_power: float32 [8, 64, 1024], P('dm', 'fft'), parts along dimension 0
There are 4 independent parts, one for each index of `dm`. A program takes and returns all parts, laid end to end along the dimension named above; an argument that names none is the same for every part. Nothing has to cross between parts.
Inputs may be any that keep to these rules, and one draw needn't show every extreme that they name: `delays`: in every even row some trial's delay is -48, in every odd row some trial's delay is 48.
All inputs are finite; a program needn't handle non-finite values.
Results may differ from a plain program's by a relative error of at most 0.0001.
Values sent between devices are 32-bit elements; how exact they have to be, the bound alone decides.
A program may use at most 64 MiB of HBM per device.

v0:
```python
import math

import jax
import jax.numpy as jnp
from jax import lax
from jax.sharding import PartitionSpec as P

ROWS = 1024
COLS = 4096
LENGTH = 4194304
ROW_SPLIT = 16
COL_SPLIT = 16
TAPS = 16
REACH = 56
HARMONICS = 8
FUND_DEV = 1024


precise_mode = lax.Precision.HIGHEST


def padded_2(cells, sides, width):
    for axis, dim in sides:
        count = lax.axis_size(axis)
        ends = count - 1
        head = lax.slice_in_dim(cells, 0, width, axis=dim)
        tail = lax.slice_in_dim(cells, cells.shape[dim] - width, cells.shape[dim], axis=dim)
        cells = jnp.concatenate(
            [
                lax.ppermute(tail, axis, [(i, (i + 1) % count) for i in range(ends)]),
                cells,
                lax.ppermute(head, axis, [((i + 1) % count, i) for i in range(ends)]),
            ],
            axis=dim,
        )
    return cells


def angle_table(first, second, length):
    product = first[:, None] * second[None, :] % length
    radians = product.astype(jnp.float32) * (-2.0 * math.pi / length)
    return (jnp.cos(radians), jnp.sin(radians))


def dft_matrix(length):
    numbers = jnp.arange(length, dtype=jnp.int32)
    return angle_table(numbers, numbers, length)


def rotate(real, imaginary, cos_part, sin_part):
    return (real * cos_part - imaginary * sin_part, real * sin_part + imaginary * cos_part)


def complex_einsum(formula, table, data):
    table_real, table_imag = table
    data_real, data_imag = data
    real = jnp.einsum(formula, table_real, data_real, precision=precise_mode)
    imaginary = jnp.einsum(formula, table_imag, data_real, precision=precise_mode)
    if data_imag is not None:
        real = real - jnp.einsum(formula, table_imag, data_imag, precision=precise_mode)
        imaginary = imaginary + jnp.einsum(formula, table_real, data_imag, precision=precise_mode)
    return (real, imaginary)


def rows_transform(real, imaginary, first_len):
    total = real.shape[0]
    second_len = total // first_len
    rest = real.shape[1:]
    shape = (first_len, second_len) + rest
    data = (real.reshape(shape), None)
    real, imaginary = complex_einsum("ru,rs...->us...", dft_matrix(first_len), data)
    cos_part, sin_part = angle_table(
        jnp.arange(first_len, dtype=jnp.int32), jnp.arange(second_len, dtype=jnp.int32), total
    )
    expand = (first_len, second_len) + (1,) * len(rest)
    real, imaginary = rotate(real, imaginary, cos_part.reshape(expand), sin_part.reshape(expand))
    real, imaginary = complex_einsum("sv,us...->vu...", dft_matrix(second_len), (real, imaginary))
    return (real.reshape((total,) + rest), imaginary.reshape((total,) + rest))


def cols_transform(real, imaginary, first_len, keep_count=None):
    total = real.shape[-1]
    second_len = total // first_len
    lead = real.shape[:-1]
    kept_blocks = -(-keep_count // first_len)
    shape = lead + (first_len, second_len)
    real, imaginary = complex_einsum(
        "ru,...rs->...us", dft_matrix(first_len), (real.reshape(shape), imaginary.reshape(shape))
    )
    cos_part, sin_part = angle_table(
        jnp.arange(first_len, dtype=jnp.int32), jnp.arange(second_len, dtype=jnp.int32), total
    )
    real, imaginary = rotate(real, imaginary, cos_part, sin_part)
    table_real, table_imag = dft_matrix(second_len)
    table = (table_real[:, :kept_blocks], table_imag[:, :kept_blocks])
    real, imaginary = complex_einsum("sv,...us->...vu", table, (real, imaginary))
    real = real.reshape(lead + (kept_blocks * first_len,))[..., :keep_count]
    imaginary = imaginary.reshape(lead + (kept_blocks * first_len,))[..., :keep_count]
    return (real, imaginary)


def taps_sum(window, taps, width):
    total = taps[..., 0:1] * window[..., 0:width]
    for step in range(1, taps.shape[-1]):
        total = total + taps[..., step : step + 1] * window[..., step : step + width]
    return total


def select_taps(filters, phases):
    selector = (phases[..., None] == jnp.arange(filters.shape[0], dtype=jnp.int32)).astype(
        jnp.float32
    )
    return jnp.einsum("...p,pt->...t", selector, filters, precision=precise_mode)


def slide_windows(source, starts, length):
    flat = jax.vmap(lambda begin: lax.dynamic_slice_in_dim(source, begin, length))(
        starts.reshape(-1)
    )
    return flat.reshape(starts.shape + (length,))


def first_section(block, own_index):
    total_rows = block.shape[0]
    width = block.shape[-1]
    columns = own_index * width + jnp.arange(width, dtype=jnp.int32)
    real, imaginary = rows_transform(block, None, ROW_SPLIT)
    rows_index = jnp.arange(total_rows, dtype=jnp.int32)
    cos_part, sin_part = angle_table(rows_index, columns, LENGTH)
    real, imaginary = rotate(
        real, imaginary, cos_part[:, None, None, :], sin_part[:, None, None, :]
    )
    return jnp.stack((real, imaginary))


def class_layout(power, limit):
    rows = power.shape[0]
    items = power.shape[1]
    needed = power.shape[3]
    ordered = jnp.transpose(power, (1, 2, 3, 0)).reshape(items, 2, needed * rows)
    return ordered[..., :limit]


def second_section(piece, parts):
    real = piece[0, :, 0]
    imaginary = piece[1, :, 0]
    limit = HARMONICS * FUND_DEV + HARMONICS
    full_rows = ROWS // parts
    needed = -(-limit // full_rows)
    scale = 1.0 / LENGTH
    out_real, out_imag = cols_transform(real, imaginary, COL_SPLIT, needed)
    power = (out_real**2 + out_imag**2) * scale
    return class_layout(power, limit)[None]


def add_harmonics(harmonic_total, power, residue, parts, fundamentals):
    trials = power.shape[0]
    for multiple in range(1, HARMONICS + 1):
        common = math.gcd(multiple, parts)
        period = parts // common
        reduced = multiple // common
        inverse = pow(reduced, -1, period)
        usable = residue % common == 0
        base = residue // common * inverse % period
        for turn in range(common):
            target = base + turn * period
            offset = jnp.clip((multiple * target - residue) // parts, 0, multiple - 1)
            strided = lax.dynamic_slice_in_dim(power, offset, multiple * fundamentals, 1)
            strided = strided.reshape(trials, fundamentals, multiple)[:, :, 0]
            term = jnp.where(usable, strided, jnp.zeros_like(strided))
            current = lax.dynamic_slice_in_dim(harmonic_total, target, 1, 1)
            harmonic_total = lax.dynamic_update_slice_in_dim(
                harmonic_total, current + term[:, None, :], target, 1
            )
    return harmonic_total


def on_device(series, filters, delays, phases):
    parts = lax.axis_size("fft")
    own_index = lax.axis_index("fft")
    trials = delays.shape[0]
    pairs = trials // 2
    local_rows = series.shape[0] // COLS
    width = COLS // parts
    padded = padded_2(series, (("fft", 0),), REACH)
    starts = REACH + jnp.arange(local_rows, dtype=jnp.int32)[:, None] * COLS + delays.T - TAPS // 2
    windows = slide_windows(padded, starts, COLS + TAPS - 1)
    taps = select_taps(filters, phases.T)
    resampled = taps_sum(windows, taps, COLS).reshape(local_rows, pairs, 2, COLS)
    spectra = (lambda block: first_section(block, own_index))(
        lax.all_to_all(resampled, "fft", split_axis=3, concat_axis=0, tiled=True)
    )
    rows_out = spectra.shape[1]
    grouped = spectra.reshape(2, rows_out // parts, parts, pairs, 2, width)
    classes = second_section(
        lax.all_to_all(grouped, "fft", split_axis=2, concat_axis=5, tiled=True), parts
    )
    residues = [own_index]
    classes = classes.reshape(len(residues), trials, classes.shape[-1])
    harmonic_total = jnp.zeros((trials, parts, FUND_DEV), jnp.float32)
    for position, residue in enumerate(residues):
        harmonic_total = add_harmonics(harmonic_total, classes[position], residue, parts, FUND_DEV)
    summed = lax.psum_scatter(harmonic_total, "fft", scatter_dimension=1, tiled=True)
    return summed * (1.0 / HARMONICS)


def solution(mesh):
    return jax.shard_map(
        on_device,
        mesh=mesh,
        in_specs=(P(("dm", "fft")), P(), P(None, "fft"), P(None, "fft")),
        out_specs=P("dm", "fft", None),
        check_vma=False,
    )
```

profile of v0, /device:TPU:1, one launch (start us, length us, event | category | flops | bytes accessed | tf_op | source)
XLA Modules:
  0.0 449.1 jit_solution(823130018291403007)
XLA Ops:
  7.3 4.9 %collective-permute-start = (f32[56]{0:T(128)S(1)}, f32[56]{0:T(128)S(1)}, u32[]{:S(2)}, u32[]{:S(2)}) collective-permute-start(f32[56]{0:T(128)S(1)} %get-tuple-element.28), channel_id=1, source_target_pairs={{0,1},{1,2},{2,3},{3,4},{4,5},{5,6},{6,7},{7,8},{8,9},{9,10},{10,1... | collective-permute-start | bytes 680 | tf_op jit(solution)/shard_map/ppermute | solution.py:30
  12.3 1.9 collective-permute-start.1
  17.4 3.1 concatenate.4
  20.4 60.1 %while.1 = (s32[]{:T(128)}, f32[65648]{0:T(1024)S(1)}, s32[32,1]{0,1:T(1,128)S(1)}, f32[32,4111]{1,0:T(8,128)S(1)}, s32[]{:T(128)}, /*index=5*/s32[]{:T(128)}) while((s32[]{:T(128)}, f32[65648]{0:T(1024)S(1)}, s32[32,1]{0,1:T(1,128)S(1)}, f32[32,4111]{1,0:T(8,128)S(1)}, s32[]{:T(128)}, /*index=5*/s32[]{:T(128)}) %tuple.50), condition=%wide.while_cond, body=%wide.while_body.sunk | while | flops 2 | bytes 98753 | solution.py:117
  80.9 9.5 %fusion.34 = f32[16,1,2,4096]{3,2,0,1:T(2,128)S(1)} fusion(f32[16,2,4111]{2,1,0:T(2,128)S(1)} %reshape.651, f32[16,2]{1,0:T(8,128)S(1)} %copy.921, f32[16,2]{1,0:T(8,128)S(1)} %copy.920, f32[16,2]{1,0:T(8,128)S(1)} %copy.919, f32[16,2]{1,0:T(8,128)S(1)} %copy.918, f32[16,2]{1,0:T(8,128)S(1)} %copy.917, f32[16,2]{1,0:T(8,128)S(1)} %copy.916, ...), kind=kLoop, calls=%fused_computation.68 | loop fusion | flops 4063232 | bytes 8914944 | tf_op jit(solution)/shard_map/reshape | solution.py:189
  90.4 4.4 copy.922
  94.8 7.9 %reshape.720 = f32[64,1,2048]{2,1,0:T(1,128)} reshape(f32[4096,1,2,16]{3,2,1,0:T(2,128)} %bitcast.185) | data formatting | bytes 1048576
  102.7 13.4 %all-to-all-start = ((f32[64,1,2048]{2,1,0:T(1,128)}), f32[64,1,2048]{2,1,0:T(1,128)S(1)}, u32[]{:S(2)}, u32[]{:S(2)}) async-start(f32[64,1,2048]{2,1,0:T(1,128)} %reshape.720), calls=%async_computation | async-start | bytes 1048576 | tf_op jit(solution)/shard_map/all_to_all | solution.py:191
  116.3 2.1 fusion.61
  118.4 14.9 %all-to-all-done = f32[64,1,2048]{2,1,0:T(1,128)S(1)} async-done(((f32[64,1,2048]{2,1,0:T(1,128)}), f32[64,1,2048]{2,1,0:T(1,128)S(1)}, u32[]{:S(2)}, u32[]{:S(2)}) %all-to-all-start) | async-done | bytes 524320 | tf_op jit(solution)/shard_map/all_to_all | solution.py:191
  133.8 1.9 reduce.32
  135.7 6.9 %reshape.721 = f32[4096,1,2,16]{3,2,1,0:T(2,128)} reshape(f32[64,2048]{1,0:T(8,128)S(1)} %reduce.32) | data formatting | bytes 1048576
  142.6 4.9 %copy.950 = f32[16,1,2,64,64]{4,0,3,2,1:T(8,128)S(1)} copy(f32[16,1,2,64,64]{0,2,4,3,1:T(2,128)} %bitcast.184) | data formatting | bytes 1048576 | tf_op jit(solution)/shard_map/all_to_all | solution.py:191
  159.4 12.0 %copy.969 = f32[2,16,64,1,2,64]{5,1,4,3,0,2:T(8,128)S(1)} copy(f32[2,16,64,1,2,64]{5,2,1,4,3,0:T(8,128)S(1)} %pad_maximum_fusion) | data formatting | bytes 2097152 | tf_op jit(solution)/shard_map/stack | solution.py:133
  171.4 2.3 reshape.722
  173.7 6.3 %all-to-all-start.1 = ((f32[64,1,4096]{2,1,0:T(1,128)}), f32[64,1,4096]{2,1,0:T(1,128)S(1)}, u32[]{:S(2)}, u32[]{:S(2)}) async-start(f32[64,1,4096]{2,1,0:T(1,128)} %reshape.722), calls=%async_computation.1 | async-start | bytes 2097152 | tf_op jit(solution)/shard_map/all_to_all | solution.py:196
  181.1 27.4 %all-to-all-done.1 = f32[64,1,4096]{2,1,0:T(1,128)S(1)} async-done(((f32[64,1,4096]{2,1,0:T(1,128)}), f32[64,1,4096]{2,1,0:T(1,128)S(1)}, u32[]{:S(2)}, u32[]{:S(2)}) %all-to-all-start.1) | async-done | bytes 1048608 | tf_op jit(solution)/shard_map/all_to_all | solution.py:196
  208.5 3.4 reduce.33
  228.4 1.9 reshape.666
  230.9 2.7 reshape.663
  234.6 2.2 fusion.19
  242.7 1.9 reshape.667
  246.5 1.9 reshape.668
  263.9 175.9 %all-reduce.3.cloned.1.call-done = f32[2,64,1024]{2,0,1:T(2,128)} async-done(((f32[2,64,1024]{2,0,1:T(2,128)}), f32[2,64,1024]{2,0,1:T(2,128)}) %all-reduce.3.cloned.1.call-update) | async-done | bytes 524304
  (288 shorter events, 119.2 us)
Async XLA Ops:
  6.5 7.7 %copy-start = (f32[32,16]{0,1:T(8,128)S(1)}, f32[32,16]{0,1:T(8,128)}, u32[]{:S(2)}) copy-start(f32[32,16]{0,1:T(8,128)} %param.5) | copy-start | bytes 6148
  7.3 10.1 %collective-permute-start = (f32[56]{0:T(128)S(1)}, f32[56]{0:T(128)S(1)}, u32[]{:S(2)}, u32[]{:S(2)}) collective-permute-start(f32[56]{0:T(128)S(1)} %get-tuple-element.28), channel_id=1, source_target_pairs={{0,1},{1,2},{2,3},{3,4},{4,5},{5,6},{6,7},{7,8},{8,9},{9,10},{10,1... | collective-permute-start | bytes 680 | tf_op jit(solution)/shard_map/ppermute | solution.py:30
  12.3 5.1 %collective-permute-start.1 = (f32[56]{0:T(128)S(1)}, f32[56]{0:T(128)S(1)}, u32[]{:S(2)}, u32[]{:S(2)}) collective-permute-start(f32[56]{0:T(128)S(1)} %get-tuple-element.27), channel_id=1, source_target_pairs={{1,0},{2,1},{3,2},{4,3},{5,4},{6,5},{7,6},{8,7},{9,8},{10,9},{11,1... | collective-permute-start | bytes 680 | tf_op jit(solution)/shard_map/ppermute | solution.py:32
  102.7 30.6 %all-to-all-start = ((f32[64,1,2048]{2,1,0:T(1,128)}), f32[64,1,2048]{2,1,0:T(1,128)S(1)}, u32[]{:S(2)}, u32[]{:S(2)}) async-start(f32[64,1,2048]{2,1,0:T(1,128)} %reshape.720), calls=%async_computation | async-start | bytes 1048576 | tf_op jit(solution)/shard_map/all_to_all | solution.py:191
  173.7 34.8 %all-to-all-start.1 = ((f32[64,1,4096]{2,1,0:T(1,128)}), f32[64,1,4096]{2,1,0:T(1,128)S(1)}, u32[]{:S(2)}, u32[]{:S(2)}) async-start(f32[64,1,4096]{2,1,0:T(1,128)} %reshape.722), calls=%async_computation.1 | async-start | bytes 2097152 | tf_op jit(solution)/shard_map/all_to_all | solution.py:196
  180.0 259.9 %all-reduce.3.cloned.1.call-start = ((), (), s32[]{:S(2)}) async-start(), calls=%async_computation.2 | async-start | bytes 1048576
  246.5 2.2 copy-start.6
  248.7 2.8 copy-start.5
  251.6 3.0 copy-start.4
  254.2 1.7 copy-start.3
  260.3 1.6 copy-start.8
  260.3 1.6 copy-start.9
  260.4 1.7 copy-start.11
  260.4 1.7 copy-start.12
  260.4 1.7 copy-start.10
  260.4 1.8 copy-start.7
  260.4 181.4 %copy-start.1 = (f32[32,16]{0,1:T(8,128)S(1)}, f32[32,16]{0,1:T(8,128)}, u32[]{:S(2)}) copy-start(f32[32,16]{0,1:T(8,128)} %param.5) | copy-start | bytes 6148
  260.8 2.6 copy-start.13
  262.5 0.8 copy-start.2
Sparse Core Ops, SparseCore 0:
  263.4 176.3 all-reduce.2
where the time goes:
time: 458 us; the launch traced here: 449 us
  waiting for transfers between devices  218 us (48%)
  local copies, waits for them, and re-layouts  139 us (30%)
  other arithmetic  30.3 us (7%)
  starting transfers between devices  26.6 us (6%)
  matrix products  18.2 us (4%)
  between operations  15.5 us (3%)
    unnamed x2, waiting for transfers between devices  176 us
    gather x128, local copies, waits for them, and re-layouts  59.2 us
    all_to_all x1, waiting for transfers between devices, on_device(): lax.all_to_all(grouped, 'fft', split_axis=2, concat_axis=5, tiled=True)  27.4 us
    reshape x19, local copies, waits for them, and re-layouts, add_harmonics(): strided = strided.reshape(trials, fundamentals, multiple)[:, :, 0]  21.5 us
    unnamed x36, local copies, waits for them, and re-layouts  21 us
    all_to_all x1, waiting for transfers between devices, on_device(): lax.all_to_all(resampled, 'fft', split_axis=3, concat_axis=0, tiled=True)  14.9 us
    all_to_all x1, starting transfers between devices, on_device(): lax.all_to_all(resampled, 'fft', split_axis=3, concat_axis=0, tiled=True)  13.4 us
    another operation x1, local copies, waits for them, and re-layouts, first_section(): return jnp.stack((real, imaginary))  12 us
  transfers between devices with their start and end apart: 5, of which 3 were waited for; matrix products, arithmetic and copies ran while one was open for 1% of the time, Pallas kernels for 0%

commit v1 on v0

v1 whole, which is shorter than its diff:
```python
import jax
import jax.numpy as jnp
import ml_dtypes
import numpy as np
from jax import lax
from jax.experimental import pallas as pl
from jax.experimental.pallas import tpu as pltpu
from jax.sharding import PartitionSpec as P

LENGTH = 4194304
SLOTS = 64
TAPS = 16
PHASES = 32
FIRST = 512
SECOND = 128
FREQS = 272
INVERSE = {1: 1, 3: 171, 5: 205, 7: 439}
BASES = {1: 0, 3: 16, 5: 32, 7: 48, 2: 64, 6: 96, 4: 128, 8: 144}
TERM_ROWS = 160


def split_table(table):
    table = np.asarray(table, np.float32)
    high = table.astype(ml_dtypes.bfloat16)
    low = (table - high.astype(np.float32)).astype(ml_dtypes.bfloat16)
    return high, low


def make_tables():
    turn = 2.0 * np.pi
    angle = turn / FIRST * (np.arange(FREQS)[:, None] * np.arange(FIRST)[None, :] % FIRST)
    first = np.concatenate([np.cos(angle), -np.sin(angle)], axis=0)
    h, a, rr, c_hi = np.meshgrid(
        np.arange(2), np.arange(2), np.arange(2), np.arange(32), indexing="ij"
    )
    second_index = (64 * rr + 2 * c_hi + h).reshape(-1)
    trial = a.reshape(-1)
    angle = turn / 65536 * (np.arange(FREQS)[:, None] * second_index[None, :] % 65536)
    mid = np.stack([np.cos(angle), -np.sin(angle)]).astype(np.float32)
    angle = turn / SECOND * (second_index[:, None] * np.arange(SECOND)[None, :] % SECOND)
    cos_part, sin_part = np.cos(angle), np.sin(angle)
    second = np.zeros((2, 256, 2, 2, SECOND))
    for t in range(2):
        own = (trial == t)[:, None]
        second[0, :, 0, t] = cos_part * own
        second[1, :, 0, t] = sin_part * own
        second[0, :, 1, t] = -sin_part * own
        second[1, :, 1, t] = cos_part * own
    second = second.reshape(512, 512)
    angle = turn / LENGTH * (np.arange(FREQS)[:, None] * np.arange(128)[None, :])
    col = np.stack([np.cos(angle), -np.sin(angle)]).astype(np.float32)
    angle = turn / 8192 * (np.arange(SLOTS)[:, None] * np.arange(SECOND)[None, :] % 8192)
    row = np.stack([np.cos(angle), -np.sin(angle)]).astype(np.float32)
    last = np.zeros((2, 2, 8, 4, 2, SLOTS, 4, 2, 2))
    special = np.zeros((2, 2, 2, 8, SLOTS, 4, 2, 2))
    q = np.arange(SLOTS)
    for sign in range(2):
        for p in range(8):
            actual = p if sign == 0 else -1 - p
            theta = turn / 64 * (q * actual % 64)
            for i in range(4):
                for t in range(2):
                    last[0, sign, p, i, t, :, i, 0, t] = np.cos(theta)
                    last[0, sign, p, i, t, :, i, 1, t] = np.sin(theta)
                    last[1, sign, p, i, t, :, i, 0, t] = -np.sin(theta)
                    last[1, sign, p, i, t, :, i, 1, t] = np.cos(theta)
            theta = turn / 128 * (q * (2 * p + sign) % 128)
            for t in range(2):
                special[0, sign, t, p, :, 0, sign, t] = np.cos(theta)
                special[1, sign, t, p, :, 0, sign, t] = -np.sin(theta)
    last = np.concatenate([last.reshape(256, 1024), special.reshape(64, 1024)], axis=0)
    return (*split_table(first), *split_table(second), *split_table(last), mid, col, row)


def split(x):
    high = x.astype(jnp.bfloat16)
    return high, (x - high.astype(jnp.float32)).astype(jnp.bfloat16)


def product(a_high, a_low, b_high, b_low):
    def dot(a, b):
        return jnp.dot(a, b, preferred_element_type=jnp.float32)

    return dot(a_high, b_high) + dot(a_low, b_high) + dot(a_high, b_low)


def lanes_at(x, index):
    return jnp.take_along_axis(x, index, axis=1, mode="promise_in_bounds")


def iota(shape, axis):
    return lax.broadcasted_iota(jnp.int32, shape, axis)


def column_of(values, own, second_trial):
    chosen = jnp.where(second_trial, values[1:2, :], values[0:1, :])
    return jnp.sum(jnp.where(own, chosen, 0.0), axis=1, keepdims=True)


def kernel(
    series, delays, phases, filters,
    first_high, first_low, second_high, second_low, last_high, last_low, mid, col, row,
    out,
    ext, responses, send1, recv1, send2, recv2, powers, rows_a, terms, received,
    v_first_high, v_first_low, v_second_high, v_second_low, v_last_high, v_last_low,
    v_mid, v_col, v_row, spectrum,
    table_sem, series_sem, halo_send, halo_recv,
    send1_sem, recv1_sem, send2_sem, recv2_sem, term_send, term_recv,
):
    me = lax.axis_index("fft")
    f32 = jnp.float32

    barrier = pltpu.get_barrier_semaphore()

    def greet(step, carry):
        pl.semaphore_signal(
            barrier, inc=1, device_id={"fft": (me + step) & (SLOTS - 1)},
            device_id_type=pl.DeviceIdType.MESH,
        )
        return carry

    lax.fori_loop(1, SLOTS, greet, 0)

    own_series = pltpu.make_async_copy(series, ext.at[pl.ds(8, 512)], series_sem)
    own_series.start()
    tables = [
        pltpu.make_async_copy(source, target, table_sem.at[n])
        for n, (source, target) in enumerate(
            (
                (first_high, v_first_high), (first_low, v_first_low),
                (second_high, v_second_high), (second_low, v_second_low),
                (last_high, v_last_high), (last_low, v_last_low),
                (mid, v_mid), (col, v_col), (row, v_row),
            )
        )
    ]
    for copy in tables:
        copy.start()

    line = iota((32, 16), 0)
    own = iota((32, 16), 1) == 2 * (line >> 2) + (line & 1)
    second_trial = ((line >> 1) & 1) == 1
    delay = column_of(delays[...].astype(f32), own, second_trial)
    phase = column_of(phases[...].astype(f32), own, second_trial)
    taps = jnp.zeros((32, TAPS), f32)
    for branch in range(PHASES):
        taps = jnp.where(phase == float(branch), filters[branch : branch + 1, :], taps)
    position = iota((32, 256), 1).astype(f32)
    response = jnp.zeros((32, 256), f32)
    for tap in range(TAPS):
        response = jnp.where(position == delay + (56.0 + tap), taps[:, tap : tap + 1], response)
    responses[...] = response

    pl.semaphore_wait(barrier, SLOTS - 1)

    @pl.when(me == 0)
    def _():
        ext[0:8, :] = jnp.zeros((8, 128), f32)

    @pl.when(me == SLOTS - 1)
    def _():
        ext[520:528, :] = jnp.zeros((8, 128), f32)

    to_next = pltpu.make_async_remote_copy(
        src_ref=series.at[pl.ds(504, 8)], dst_ref=ext.at[pl.ds(0, 8)],
        send_sem=halo_send.at[0], recv_sem=halo_recv.at[0],
        device_id={"fft": (me + 1) & (SLOTS - 1)}, device_id_type=pl.DeviceIdType.MESH,
    )
    to_last = pltpu.make_async_remote_copy(
        src_ref=series.at[pl.ds(0, 8)], dst_ref=ext.at[pl.ds(520, 8)],
        send_sem=halo_send.at[1], recv_sem=halo_recv.at[1],
        device_id={"fft": (me + SLOTS - 1) & (SLOTS - 1)}, device_id_type=pl.DeviceIdType.MESH,
    )

    @pl.when(me < SLOTS - 1)
    def _():
        to_next.start()

    @pl.when(me > 0)
    def _():
        to_last.start()

    own_series.wait()

    @pl.when(me > 0)
    def _():
        to_next.wait_recv()

    @pl.when(me < SLOTS - 1)
    def _():
        to_last.wait_recv()

    lane = iota((64, 128), 1)
    block_of = iota((128, 128), 1) >> 5

    def resample(rg, carry):
        before = ext[pl.ds(64 * rg + 7, 64), :]
        here = ext[pl.ds(pl.multiple_of(64 * rg + 8, 8), 64), :]
        after = ext[pl.ds(64 * rg + 9, 64), :]
        left = pltpu.roll(jnp.where(lane < 64, here, before), 64, 1)
        right = pltpu.roll(jnp.where(lane < 64, after, here), 64, 1)
        window = jnp.concatenate(
            [jnp.concatenate([left, left], 0).T, jnp.concatenate([right, right], 0).T], 0
        )
        w_high, w_low = split(window)
        total = jnp.zeros((128, 128), f32)
        for block in range(4):
            line = responses[pl.ds(4 * rg + block, 1), :]
            band = pltpu.roll(jnp.broadcast_to(line, (128, 256)), 0, 1, stride=1, stride_axis=0)
            b_high, b_low = split(band)
            total = jnp.where(block_of == block, product(b_high, b_low, w_high, w_low), total)
        send1[pl.ds(rg, 64, stride=16), :] = total[0:64]
        send1[pl.ds(8 + rg, 64, stride=16), :] = total[64:128]
        return carry

    lax.fori_loop(0, 8, resample, 0)

    def exchange(source, target, send_sem, recv_sem):
        mine = pl.ds(pl.multiple_of(16 * me, 16), 16)

        def send(step, carry):
            to = (me + step) & (SLOTS - 1)
            pltpu.make_async_remote_copy(
                src_ref=source.at[pl.ds(pl.multiple_of(16 * to, 16), 16)],
                dst_ref=target.at[mine],
                send_sem=send_sem, recv_sem=recv_sem,
                device_id={"fft": to}, device_id_type=pl.DeviceIdType.MESH,
            ).start()
            return carry

        lax.fori_loop(1, SLOTS, send, 0)
        pltpu.make_async_copy(source.at[mine], target.at[mine], recv_sem).start()

    def arrived(target, sem):
        pltpu.make_async_copy(target, target, sem).wait()

    def sent(source, sem):
        part = source.at[pl.ds(0, 16 * (SLOTS - 1))]
        pltpu.make_async_copy(part, part, sem).wait()

    exchange(send1, recv1, send1_sem, recv1_sem)
    for copy in tables:
        copy.wait()
    me_lane = iota((FREQS, 128), 1) == me
    col_cos = jnp.sum(jnp.where(me_lane, v_col[0], 0.0), axis=1, keepdims=True)
    col_sin = jnp.sum(jnp.where(me_lane, v_col[1], 0.0), axis=1, keepdims=True)
    row_cos = v_row[0, pl.ds(me, 1), :]
    row_sin = v_row[1, pl.ds(me, 1), :]
    turn_cos = col_cos * row_cos - col_sin * row_sin
    turn_sin = col_cos * row_sin + col_sin * row_cos
    arrived(recv1, recv1_sem)

    block = recv1[...].reshape(SLOTS, 2, 8, 128)
    data = jnp.concatenate(
        [block[:, 0].reshape(FIRST, 128), block[:, 1].reshape(FIRST, 128)], 1
    )
    d_high, d_low = split(data)
    spectrum[...] = product(v_first_high[...], v_first_low[...], d_high, d_low)
    real, imaginary = spectrum[0:FREQS, :], spectrum[FREQS : 2 * FREQS, :]
    mid_cos, mid_sin = v_mid[0], v_mid[1]
    turned = jnp.concatenate(
        [real * mid_cos - imaginary * mid_sin, real * mid_sin + imaginary * mid_cos], 1
    )
    t_high, t_low = split(turned)
    result = product(t_high, t_low, v_second_high[...], v_second_low[...])
    lane1 = iota((1, 128), 1)
    for t in range(2):
        real = result[:, 128 * t : 128 * t + 128]
        imaginary = result[:, 256 + 128 * t : 384 + 128 * t]
        parts = (
            real * turn_cos - imaginary * turn_sin,
            real * turn_sin + imaginary * turn_cos,
        )
        middle = pltpu.roll(real[0:1], 64, 1)
        for c in range(2):
            for i in range(4):
                send2[pl.ds(4 * i + 2 * c + t, 64, stride=16), :] = parts[c][64 * i : 64 * i + 64]
            packed = jnp.where(lane1 < 64, parts[c][0:1], pltpu.roll(parts[c][256:257], 64, 1))
            if c == 1:
                packed = jnp.where(lane1 == 0, middle, packed)
            send2[2 * c + t : 2 * c + t + 1, :] = packed

    exchange(send2, recv2, send2_sem, recv2_sem)
    arrived(recv2, recv2_sem)

    r_high, r_low = split(recv2[...])
    final = product(v_last_high[...], v_last_low[...], r_high, r_low)
    power = final[0:128] ** 2 + final[128:256] ** 2
    special = final[256:288] ** 2 + final[288:320] ** 2
    powers[...] = power
    lane8, sub8 = iota((8, 128), 1), iota((8, 128), 0)

    @pl.when(me == 0)
    def _():
        for sign in range(2):
            for t in range(2):
                where = pl.ds(64 * sign + t, 8, stride=8)
                at = 16 * sign + 8 * t
                powers[where, :] = jnp.where(lane8 == 0, special[at : at + 8], powers[where, :])
        for p in range(8):
            plus = powers[8 * p : 8 * p + 8, :]
            minus = powers[64 + 8 * p : 72 + 8 * p, :]
            head = sub8 < 2
            powers[8 * p : 8 * p + 8, :] = jnp.where(
                head & (lane8 >= 64), lanes_at(minus, (128 - lane8) & 63), plus
            )
            index = jnp.where(head, 191 - lane8, 127 - lane8) & 127
            turned = jnp.where(
                head & (lane8 < 64), lanes_at(plus, (lane8 + 64) & 127), lanes_at(minus, index)
            )
            powers[64 + 8 * p : 72 + 8 * p, :] = pltpu.roll(turned, 6, 0)

    @pl.when(me != 0)
    def _():
        for p in range(8):
            minus = powers[64 + 8 * p : 72 + 8 * p, :]
            powers[64 + 8 * p : 72 + 8 * p, :] = lanes_at(minus, 127 - lane8)

    for sign in range(2):
        for i in range(4):
            for t in range(2):
                rows_a[pl.ds(64 * sign + 16 * i + t, 8, stride=2), :] = powers[
                    pl.ds(64 * sign + 2 * i + t, 8, stride=8), :
                ]

    def residue(sign):
        return me if sign == 0 else (SLOTS - me) & (SLOTS - 1)

    def select(sign, m, odd, share, half):
        slot = sub8 >> 1
        place = slot if sign == 0 else 7 - slot
        k1 = (INVERSE[odd] * ((residue(sign) + 64 * place) // share)) & (FIRST // share - 1)
        index = ((m * k1) >> 9) + odd * (128 * half + lane8)
        total = jnp.zeros((8, 128), f32)
        for p in range(odd * half, odd * half + odd):
            at = 64 * sign + 8 * p
            total = jnp.where(
                (index >> 7) == p, lanes_at(powers[at : at + 8, :], index & 127), total
            )
        return total

    started = []

    def give(source, start, m, sign, rows, to, condition):
        base = BASES[m] + (0 if m == 8 else rows * sign)
        from_ref = source.at[pl.ds(start, rows)]
        to_ref = received.at[pl.ds(base, rows)]
        number = len(started)
        copy = pltpu.make_async_remote_copy(
            src_ref=from_ref, dst_ref=to_ref,
            send_sem=term_send.at[number], recv_sem=term_recv,
            device_id={"fft": to}, device_id_type=pl.DeviceIdType.MESH,
        )
        away = condition & (to != me)

        @pl.when(away)
        def _():
            copy.start()

        @pl.when(condition & (to == me))
        def _():
            pltpu.make_async_copy(from_ref, to_ref, term_recv).start()

        started.append((copy, away))

    for sign in range(2):
        rest = residue(sign)
        always = me >= 0
        even = (me & 1) == 0
        give(powers, 64 * sign, 1, sign, 8, rest, always)
        for v in range(2):
            give(powers, 64 * sign, 2, sign, 16, ((rest >> 1) + 32 * v) & 63, even)
        for i in range(4):
            place = i if sign == 0 else 7 - i
            give(rows_a, 64 * sign + 16 * i, 4, sign, 8, ((rest >> 2) + 16 * place) & 63, (me & 3) == 0)
            give(rows_a, 64 * sign + 16 * i, 8, sign, 16, ((rest >> 3) + 8 * place) & 63, (me & 7) == 0)
    for n, m in enumerate((3, 5, 7)):
        for sign in range(2):
            at = 16 * n + 8 * sign
            terms[at : at + 8, :] = select(sign, m, m, 1, 0)
            give(terms, at, m, sign, 8, (INVERSE[m] * residue(sign)) & 63, me >= 0)
    for sign in range(2):
        for half in range(2):
            at = 48 + 16 * sign + 8 * half
            terms[at : at + 8, :] = select(sign, 6, 3, 2, half)
        for v in range(2):
            to = (INVERSE[3] * ((residue(sign) >> 1) + 32 * v)) & 63
            give(terms, 48 + 16 * sign, 6, sign, 16, to, (me & 1) == 0)

    arrived(received, term_recv)

    def source_row(m, v, rows):
        place = (((m * me) >> 6) + m * v) & 7
        sign = place >> 2
        slot = jnp.where(sign == 1, 7 - place, place)
        return BASES[m] + rows * sign + 2 * slot

    for t in range(2):
        total = received[pl.ds(BASES[8] + t, 8, stride=2), :]
        for v in range(2):
            base = BASES[4] + 8 * v + t
            values = jnp.broadcast_to(received[base : base + 1, :], (8, 128))
            for p in range(1, 4):
                values = jnp.where((sub8 >> 1) == p, received[base + 2 * p : base + 2 * p + 1, :], values)
            values = lanes_at(values, 64 * (sub8 & 1) + (lane8 >> 1))
            total = total + jnp.where((lane8 & 1) == v, values, 0.0)
        for v in range(4):
            at2 = source_row(2, v, 16) + t
            at6 = source_row(6, v, 16) + t
            low = received[pl.ds(at2, 1), :] + received[pl.ds(at6, 1), :]
            high = received[pl.ds(at2 + 8, 1), :] + received[pl.ds(at6 + 8, 1), :]
            values = jnp.where((sub8 >> 2) == 0, low, high)
            values = lanes_at(values, 32 * (sub8 & 3) + (lane8 >> 2))
            total = total + jnp.where((lane8 & 3) == v, values, 0.0)
        for v in range(8):
            values = received[pl.ds(source_row(1, v, 8) + t, 1), :]
            for m in (3, 5, 7):
                values = values + received[pl.ds(source_row(m, v, 8) + t, 1), :]
            values = lanes_at(jnp.broadcast_to(values, (8, 128)), 16 * sub8 + (lane8 >> 3))
            total = total + jnp.where((lane8 & 7) == v, values, 0.0)
        out[t] = total * (0.125 / LENGTH)

    @pl.when(me < SLOTS - 1)
    def _():
        to_next.wait_send()

    @pl.when(me > 0)
    def _():
        to_last.wait_send()

    sent(send1, send1_sem)
    sent(send2, send2_sem)
    for copy, away in started:

        @pl.when(away)
        def _(copy=copy):
            copy.wait_send()


def on_device(series, filters, delays, phases):
    tables = [jnp.asarray(table) for table in make_tables()]
    whole = pl.BlockSpec(memory_space=pltpu.VMEM)
    anywhere = pl.BlockSpec(memory_space=pl.ANY)
    f32 = jnp.float32
    out = pl.pallas_call(
        kernel,
        out_shape=jax.ShapeDtypeStruct((2, 8, 128), f32),
        in_specs=[anywhere, whole, whole, whole] + [anywhere] * len(tables),
        out_specs=whole,
        scratch_shapes=[
            pltpu.VMEM((528, 128), f32),
            pltpu.VMEM((32, 256), f32),
            pltpu.VMEM((1024, 128), f32),
            pltpu.VMEM((1024, 128), f32),
            pltpu.VMEM((1024, 128), f32),
            pltpu.VMEM((1024, 128), f32),
            pltpu.VMEM((128, 128), f32),
            pltpu.VMEM((128, 128), f32),
            pltpu.VMEM((80, 128), f32),
            pltpu.VMEM((TERM_ROWS, 128), f32),
        ]
        + [pltpu.VMEM(table.shape, table.dtype) for table in tables]
        + [
            pltpu.VMEM((2 * FREQS, 256), f32),
            pltpu.SemaphoreType.DMA((len(tables),)),
            pltpu.SemaphoreType.DMA,
            pltpu.SemaphoreType.DMA((2,)),
            pltpu.SemaphoreType.DMA((2,)),
            pltpu.SemaphoreType.DMA,
            pltpu.SemaphoreType.DMA,
            pltpu.SemaphoreType.DMA,
            pltpu.SemaphoreType.DMA,
            pltpu.SemaphoreType.DMA((32,)),
            pltpu.SemaphoreType.DMA,
        ],
        compiler_params=pltpu.CompilerParams(
            collective_id=0, has_side_effects=True, vmem_limit_bytes=48 * 1024 * 1024
        ),
    )(series.reshape(512, 128), delays, phases, filters, *tables)
    return out.reshape(2, 1, 1024)


def solution(mesh):
    return jax.shard_map(
        on_device,
        mesh=mesh,
        in_specs=(P(("dm", "fft")), P(), P(None, "fft"), P(None, "fft")),
        out_specs=P("dm", "fft", None),
        check_vma=False,
    )
```

time: 458 us -> 69.8 us (0.15); the launches traced: 449 us -> 69.3 us
  waiting for transfers between devices: 218 us -> 0 us
  local copies, waits for them, and re-layouts: 139 us -> 11.6 us
  Pallas kernels: 0 us -> 57.7 us
  other arithmetic: 30.3 us -> 0 us
  starting transfers between devices: 26.6 us -> 0 us
  matrix products: 18.2 us -> 0 us
  between operations: 15.5 us -> 0.03 us
    unnamed x2 -> x0, waiting for transfers between devices: 176 us -> none
    gather x128 -> x0, local copies, waits for them, and re-layouts: 59.2 us -> none
    pallas_call x0 -> x1, Pallas kernels: none -> 57.7 us  [on_device(): pl.pallas_call(kernel, out_shape=jax.ShapeDtypeStruct((2, 8, 128), f32),...]
    all_to_all x2 -> x0, waiting for transfers between devices: 42.3 us -> none  [the longest x1 27.4 us: on_device(): lax.all_to_all(grouped, 'fft', split_axis=2, concat_axis=5, tiled=True)]
    reshape x25 -> x0, local copies, waits for them, and re-layouts: 26.9 us -> none  [the longest x19 21.5 us: add_harmonics(): strided = strided.reshape(trials, fundamentals, multiple)[:, :, 0]]
    all_to_all x2 -> x0, starting transfers between devices: 19.7 us -> none  [the longest x1 13.4 us: on_device(): lax.all_to_all(resampled, 'fft', split_axis=3, concat_axis=0, tiled=True)]
    dot_general x15 -> x0, matrix products: 18.2 us -> none  [the longest x4 5.27 us: complex_einsum(): real = jnp.einsum(formula, table_real, data_real, precision=precise_mode)]
    another operation x3 -> x0, local copies, waits for them, and re-layouts: 12.5 us -> none  [the longest x1 12 us: first_section(): return jnp.stack((real, imaginary))]
  transfers between devices with their start and end apart: 5 -> 0, of which waited for: 3 -> 0; matrix products, arithmetic and copies ran while one was open for 1% -> 0% of each run, Pallas kernels for 0% -> 0%
where the time goes in v1:
time: 69.8 us; the launch traced here: 69.3 us
  Pallas kernels  57.7 us (83%)
  local copies, waits for them, and re-layouts  11.6 us (17%)
    pallas_call x1, Pallas kernels, on_device(): pl.pallas_call(kernel, out_shape=jax.ShapeDtypeStruct((2, 8, 128), f32),...  57.7 us
    unnamed x26, local copies, waits for them, and re-layouts  11.6 us

profile of v1, /device:TPU:1, one launch (start us, length us, event | category | flops | bytes accessed | tf_op | source)
XLA Modules:
  0.0 69.3 jit_solution(7884452656253101363)
XLA Ops:
  0.0 0.0 copy-start.10
  0.0 0.0 copy-start.11
  0.0 0.8 %copy.14.filters = f32[32,16]{1,0:T(8,128)S(1)} copy(f32[32,16]{0,1:T(8,128)} %param.14) | data formatting | bytes 4096 | tf_op args[1]
  0.8 0.0 copy-done.10
  0.8 0.0 copy-done.11
  0.8 0.0 copy-start
  0.8 1.1 %copy-done = bf16[320,1024]{1,0:T(8,128)(2,1)S(1)} copy-done((bf16[320,1024]{1,0:T(8,128)(2,1)S(1)}, bf16[320,1024]{1,0:T(8,128)(2,1)}, u32[]{:S(2)}) %copy-start) | copy-done | bytes 655384
  1.9 0.0 copy-start.1
  1.9 1.1 %copy-done.1 = bf16[320,1024]{1,0:T(8,128)(2,1)S(1)} copy-done((bf16[320,1024]{1,0:T(8,128)(2,1)S(1)}, bf16[320,1024]{1,0:T(8,128)(2,1)}, u32[]{:S(2)}) %copy-start.1) | copy-done | bytes 655384
  3.0 0.0 copy-start.2
  3.0 1.1 %copy-done.2 = f32[2,272,256]{2,1,0:T(8,128)S(1)} copy-done((f32[2,272,256]{2,1,0:T(8,128)S(1)}, f32[2,272,256]{2,1,0:T(8,128)}, u32[]{:S(2)}) %copy-start.2) | copy-done | bytes 557080
  4.0 0.0 copy-start.3
  4.0 1.1 %copy-done.3 = bf16[544,512]{1,0:T(8,128)(2,1)S(1)} copy-done((bf16[544,512]{1,0:T(8,128)(2,1)S(1)}, bf16[544,512]{1,0:T(8,128)(2,1)}, u32[]{:S(2)}) %copy-start.3) | copy-done | bytes 557080
  5.1 1.1 %copy-done.4 = bf16[544,512]{1,0:T(8,128)(2,1)S(1)} copy-done((bf16[544,512]{1,0:T(8,128)(2,1)S(1)}, bf16[544,512]{1,0:T(8,128)(2,1)}, u32[]{:S(2)}) %copy-start.4) | copy-done | bytes 557080
  6.1 0.0 copy-start.5
  6.2 1.0 %copy-done.5 = bf16[512,512]{1,0:T(8,128)(2,1)S(1)} copy-done((bf16[512,512]{1,0:T(8,128)(2,1)S(1)}, bf16[512,512]{1,0:T(8,128)(2,1)}, u32[]{:S(2)}) %copy-start.5) | copy-done | bytes 524312
  7.2 0.0 copy-start.6
  7.2 1.0 %copy-done.6 = bf16[512,512]{1,0:T(8,128)(2,1)S(1)} copy-done((bf16[512,512]{1,0:T(8,128)(2,1)S(1)}, bf16[512,512]{1,0:T(8,128)(2,1)}, u32[]{:S(2)}) %copy-start.6) | copy-done | bytes 524312
  8.2 0.0 copy-start.7
  8.2 1.0 %copy-done.7 = f32[2,272,128]{2,1,0:T(8,128)S(1)} copy-done((f32[2,272,128]{2,1,0:T(8,128)S(1)}, f32[2,272,128]{2,1,0:T(8,128)}, u32[]{:S(2)}) %copy-start.7) | copy-done | bytes 278552
  9.2 0.9 %copy-done.8 = f32[65536]{0:T(1024)S(1)} copy-done((f32[65536]{0:T(1024)S(1)}, f32[65536]{0:T(1024)}, u32[]{:S(2)}) %copy-start.8) | copy-done | bytes 262168
  10.1 0.8 %copy-done.9 = f32[2,64,128]{2,1,0:T(8,128)S(1)} copy-done((f32[2,64,128]{2,1,0:T(8,128)S(1)}, f32[2,64,128]{2,1,0:T(8,128)}, u32[]{:S(2)}) %copy-start.9) | copy-done | bytes 65560
  11.0 57.7 %shard_map.127 = f32[2,8,128]{2,1,0:T(8,128)S(1)} custom-call(f32[512,128]{1,0:T(8,128)S(1)} %bitcast.2, s32[2,16]{1,0:T(2,128)S(1)} %copy-done.10, s32[2,16]{1,0:T(2,128)S(1)} %copy-done.11, f32[32,16]{1,0:T(8,128)S(1)} %copy.14.filters, bf16[544,512]{1,0:T(8,128)(2,1)S(1)} %copy-done.4, bf16[544,512]{1,0:T(8,128)(2,1)S(1)} %copy-done.3, ...), custom_call_target="tpu_custom_call" | custom-call | tf_op jit(solution)/shard_map/pallas_call | solution.py:445
  68.7 0.6 copy.17
  (3 shorter events, 0.0 us)
Async XLA Ops:
  0.0 0.8 %copy-start.10 = (s32[2,16]{1,0:T(2,128)S(1)}, s32[2,16]{1,0:T(2,128)}, u32[]{:S(2)}) copy-start(s32[2,16]{1,0:T(2,128)} %delays.1) | copy-start | bytes 388
  0.0 0.8 %copy-start.11 = (s32[2,16]{1,0:T(2,128)S(1)}, s32[2,16]{1,0:T(2,128)}, u32[]{:S(2)}) copy-start(s32[2,16]{1,0:T(2,128)} %phases.1) | copy-start | bytes 388
  0.8 1.1 %copy-start = (bf16[320,1024]{1,0:T(8,128)(2,1)S(1)}, bf16[320,1024]{1,0:T(8,128)(2,1)}, u32[]{:S(2)}) copy-start(bf16[320,1024]{1,0:T(8,128)(2,1)} %constant.23.clone.last_low) | copy-start | bytes 1966084
  1.9 1.1 %copy-start.1 = (bf16[320,1024]{1,0:T(8,128)(2,1)S(1)}, bf16[320,1024]{1,0:T(8,128)(2,1)}, u32[]{:S(2)}) copy-start(bf16[320,1024]{1,0:T(8,128)(2,1)} %constant.22.clone.last_high) | copy-start | bytes 1966084
  3.0 1.1 %copy-start.2 = (f32[2,272,256]{2,1,0:T(8,128)S(1)}, f32[2,272,256]{2,1,0:T(8,128)}, u32[]{:S(2)}) copy-start(f32[2,272,256]{2,1,0:T(8,128)} %constant.24.clone.mid) | copy-start | bytes 1671172
  4.0 1.1 %copy-start.3 = (bf16[544,512]{1,0:T(8,128)(2,1)S(1)}, bf16[544,512]{1,0:T(8,128)(2,1)}, u32[]{:S(2)}) copy-start(bf16[544,512]{1,0:T(8,128)(2,1)} %constant.19.clone.first_low) | copy-start | bytes 1671172
  5.1 1.1 %copy-start.4 = (bf16[544,512]{1,0:T(8,128)(2,1)S(1)}, bf16[544,512]{1,0:T(8,128)(2,1)}, u32[]{:S(2)}) copy-start(bf16[544,512]{1,0:T(8,128)(2,1)} %constant.18.clone.first_high) | copy-start | bytes 1671172
  6.1 1.0 %copy-start.5 = (bf16[512,512]{1,0:T(8,128)(2,1)S(1)}, bf16[512,512]{1,0:T(8,128)(2,1)}, u32[]{:S(2)}) copy-start(bf16[512,512]{1,0:T(8,128)(2,1)} %constant.21.clone.second_low) | copy-start | bytes 1572868
  7.2 1.0 %copy-start.6 = (bf16[512,512]{1,0:T(8,128)(2,1)S(1)}, bf16[512,512]{1,0:T(8,128)(2,1)}, u32[]{:S(2)}) copy-start(bf16[512,512]{1,0:T(8,128)(2,1)} %constant.20.clone.second_high) | copy-start | bytes 1572868
  8.2 1.0 %copy-start.7 = (f32[2,272,128]{2,1,0:T(8,128)S(1)}, f32[2,272,128]{2,1,0:T(8,128)}, u32[]{:S(2)}) copy-start(f32[2,272,128]{2,1,0:T(8,128)} %constant.25.clone.col) | copy-start | bytes 835588
  9.2 0.9 %copy-start.8 = (f32[65536]{0:T(1024)S(1)}, f32[65536]{0:T(1024)}, u32[]{:S(2)}) copy-start(f32[65536]{0:T(1024)} %param.13) | copy-start | bytes 786436
  10.1 0.8 %copy-start.9 = (f32[2,64,128]{2,1,0:T(8,128)S(1)}, f32[2,64,128]{2,1,0:T(8,128)}, u32[]{:S(2)}) copy-start(f32[2,64,128]{2,1,0:T(8,128)} %constant.26.clone.row) | copy-start | bytes 196612

commit v2 on v1

v2 whole, which is shorter than its diff:
```python
import jax
import jax.numpy as jnp
import ml_dtypes
import numpy as np
from jax import lax
from jax.experimental import pallas as pl
from jax.experimental.pallas import tpu as pltpu
from jax.sharding import PartitionSpec as P

LENGTH = 4194304
SLOTS = 64
TAPS = 16
PHASES = 32
FIRST = 512
SECOND = 128
FREQS = 272
INVERSE = {1: 1, 3: 171, 5: 205, 7: 439}
BASES = {1: 0, 3: 16, 5: 32, 7: 48, 2: 64, 6: 96, 4: 128, 8: 144}
TERM_ROWS = 152


def split_table(table):
    table = np.asarray(table, np.float32)
    high = table.astype(ml_dtypes.bfloat16)
    low = (table - high.astype(np.float32)).astype(ml_dtypes.bfloat16)
    return high, low


def make_tables():
    turn = 2.0 * np.pi
    angle = turn / FIRST * (np.arange(FREQS)[:, None] * np.arange(FIRST)[None, :] % FIRST)
    first = np.concatenate([np.cos(angle), -np.sin(angle)], axis=0)
    h, rr, c_hi = np.meshgrid(np.arange(2), np.arange(2), np.arange(32), indexing="ij")
    second_index = (64 * rr + 2 * c_hi + h).reshape(-1)
    angle = turn / 65536 * (np.arange(FREQS)[:, None] * second_index[None, :] % 65536)
    mid = np.stack([np.cos(angle), -np.sin(angle)]).astype(np.float32)
    angle = turn / SECOND * (second_index[:, None] * np.arange(SECOND)[None, :] % SECOND)
    cos_part, sin_part = np.cos(angle), np.sin(angle)
    second = np.block([[cos_part, -sin_part], [sin_part, cos_part]])
    angle = turn / LENGTH * (np.arange(FREQS)[:, None] * np.arange(128)[None, :])
    col = np.stack([np.cos(angle), -np.sin(angle)]).astype(np.float32)
    angle = turn / 8192 * (np.arange(SLOTS)[:, None] * np.arange(SECOND)[None, :] % 8192)
    row = np.stack([np.cos(angle), -np.sin(angle)]).astype(np.float32)
    last = np.zeros((2, 8, 2, 4, SLOTS, 4, 2))
    special = np.zeros((2, 2, 8, SLOTS, 4, 2))
    q = np.arange(SLOTS)
    for sign in range(2):
        for p in range(8):
            actual = p if sign == 0 else -1 - p
            theta = turn / 64 * (q * actual % 64)
            for i in range(4):
                last[0, p, sign, i, :, i, 0] = np.cos(theta)
                last[0, p, sign, i, :, i, 1] = np.sin(theta)
                last[1, p, sign, i, :, i, 0] = -np.sin(theta)
                last[1, p, sign, i, :, i, 1] = np.cos(theta)
            theta = turn / 128 * (q * (2 * p + sign) % 128)
            special[0, sign, p, :, 0, sign] = np.cos(theta)
            special[1, sign, p, :, 0, sign] = -np.sin(theta)
    last = np.concatenate([last.reshape(128, 512), special.reshape(32, 512)], axis=0)
    return (*split_table(first), *split_table(second), *split_table(last), mid, col, row)


def split(x):
    high = x.astype(jnp.bfloat16)
    return high, (x - high.astype(jnp.float32)).astype(jnp.bfloat16)


def dot(a, b):
    return jnp.dot(a, b, preferred_element_type=jnp.float32)


def product(a_high, a_low, b_high, b_low):
    wide = dot(a_high, jnp.concatenate([b_high, b_low], 1))
    return wide[:, 0:128] + wide[:, 128:256] + dot(a_low, b_high)


def lanes_at(x, index):
    return jnp.take_along_axis(x, index, axis=1, mode="promise_in_bounds")


def iota(shape, axis):
    return lax.broadcasted_iota(jnp.int32, shape, axis)


def column_of(values, own, second_trial):
    chosen = jnp.where(second_trial, values[1:2, :], values[0:1, :])
    return jnp.sum(jnp.where(own, chosen, 0.0), axis=1, keepdims=True)


def kernel(
    series, delays, phases, filters,
    first_high, first_low, second_high, second_low, last_high, last_low, mid, col, row,
    out,
    ext, responses, windows_high, windows_low, send1, recv1, send2, recv2, spectrum, turn,
    powers, rows_a, terms, received,
    v_first_high, v_first_low, v_second_high, v_second_low, v_last_high, v_last_low,
    v_mid, v_col, v_row,
    table_sem, series_sem, halo_send, halo_recv,
    send1_sem, recv1_sem, send2_sem, recv2_sem, term_send, term_recv,
):
    me = lax.axis_index("fft")
    f32 = jnp.float32
    mesh_id = pl.DeviceIdType.MESH

    barrier = pltpu.get_barrier_semaphore()

    def greet(step, carry):
        pl.semaphore_signal(
            barrier, inc=1, device_id={"fft": (me + step) & (SLOTS - 1)}, device_id_type=mesh_id
        )
        return carry

    lax.fori_loop(1, SLOTS, greet, 0)

    own_series = pltpu.make_async_copy(series, ext.at[pl.ds(8, 512)], series_sem)
    own_series.start()
    tables = [
        pltpu.make_async_copy(source, target, table_sem.at[n])
        for n, (source, target) in enumerate(
            (
                (first_high, v_first_high), (first_low, v_first_low),
                (second_high, v_second_high), (second_low, v_second_low),
                (last_high, v_last_high), (last_low, v_last_low),
                (mid, v_mid), (col, v_col), (row, v_row),
            )
        )
    ]
    for copy in tables:
        copy.start()

    line = iota((32, 16), 0)
    own = iota((32, 16), 1) == 2 * (line >> 2) + (line & 1)
    second_trial = ((line >> 1) & 1) == 1
    delay = column_of(delays[...].astype(f32), own, second_trial)
    phase = column_of(phases[...].astype(f32), own, second_trial)
    branch = (iota((32, PHASES), 1).astype(f32) == phase).astype(f32)
    taps = lax.dot_general(
        branch, filters[...], (((1,), (1,)), ((), ())),
        precision=lax.Precision.HIGHEST, preferred_element_type=f32,
    )
    position = iota((32, 256), 1).astype(f32) - (delay + 56.0)
    response = jnp.zeros((32, 256), f32)
    for tap in range(TAPS):
        response = jnp.where(position == float(tap), taps[:, tap : tap + 1], response)
    responses[...] = response

    pl.semaphore_wait(barrier, SLOTS - 1)
    to_next = pltpu.make_async_remote_copy(
        src_ref=series.at[pl.ds(504, 8)], dst_ref=ext.at[pl.ds(0, 8)],
        send_sem=halo_send.at[0], recv_sem=halo_recv.at[0],
        device_id={"fft": (me + 1) & (SLOTS - 1)}, device_id_type=mesh_id,
    )
    to_last = pltpu.make_async_remote_copy(
        src_ref=series.at[pl.ds(0, 8)], dst_ref=ext.at[pl.ds(520, 8)],
        send_sem=halo_send.at[1], recv_sem=halo_recv.at[1],
        device_id={"fft": (me + SLOTS - 1) & (SLOTS - 1)}, device_id_type=mesh_id,
    )

    @pl.when(me < SLOTS - 1)
    def _():
        to_next.start()

    @pl.when(me > 0)
    def _():
        to_last.start()

    own_series.wait()

    lane64 = iota((64, 128), 1)
    quarter = lane64 >> 5

    def resample(trial, rg):
        if trial == 0:
            before = ext[pl.ds(64 * rg + 7, 64), :]
            here = ext[pl.ds(64 * rg + 8, 64), :]
            after = ext[pl.ds(64 * rg + 9, 64), :]
            left = pltpu.roll(jnp.where(lane64 < 64, here, before), 64, 1)
            right = pltpu.roll(jnp.where(lane64 < 64, after, here), 64, 1)
            window = jnp.concatenate(
                [jnp.concatenate([left, left], 0).T, jnp.concatenate([right, right], 0).T], 0
            )
            w_high, w_low = split(window)
            windows_high[rg], windows_low[rg] = w_high, w_low
        else:
            w_high, w_low = windows_high[rg], windows_low[rg]
        bands = []
        for rr in range(2):
            line = responses[pl.ds(4 * rg + 2 * trial + rr, 1), :]
            bands.append(
                pltpu.roll(jnp.broadcast_to(line, (128, 256)), 0, 1, stride=1, stride_axis=0)
            )
        b_high, b_low = split(jnp.concatenate(bands, 0))
        both = product(b_high, b_low, w_high, w_low)
        total = jnp.where((quarter & 1) == 0, both[0:64], both[128:192])
        later = jnp.where((quarter & 1) == 0, both[64:128], both[192:256])
        send1[trial, pl.ds(rg, 64, stride=8), :] = jnp.where(quarter < 2, total, later)

    def exchange(source, target, send_sem, recv_sem):
        mine = pl.ds(pl.multiple_of(8 * me, 8), 8)

        def send(step, carry):
            to = (me + step) & (SLOTS - 1)
            pltpu.make_async_remote_copy(
                src_ref=source.at[pl.ds(pl.multiple_of(8 * to, 8), 8)],
                dst_ref=target.at[mine],
                send_sem=send_sem, recv_sem=recv_sem,
                device_id={"fft": to}, device_id_type=mesh_id,
            ).start()
            return carry

        lax.fori_loop(1, SLOTS, send, 0)
        pltpu.make_async_copy(source.at[mine], target.at[mine], recv_sem).start()

    def arrived(target, sem):
        pltpu.make_async_copy(target, target, sem).wait()

    def sent(source, sem):
        part = source.at[pl.ds(0, 8 * (SLOTS - 1))]
        pltpu.make_async_copy(part, part, sem).wait()

    def inner(trial):
        def body(rg, carry):
            resample(trial, rg)
            return carry

        return body

    lax.fori_loop(1, 7, inner(0), 0)

    @pl.when(me > 0)
    def _():
        to_next.wait_recv()

    @pl.when(me == 0)
    def _():
        ext[0:8, :] = jnp.zeros((8, 128), f32)

    @pl.when(me < SLOTS - 1)
    def _():
        to_last.wait_recv()

    @pl.when(me == SLOTS - 1)
    def _():
        ext[520:528, :] = jnp.zeros((8, 128), f32)

    resample(0, 0)
    resample(0, 7)
    exchange(send1.at[0], recv1.at[0], send1_sem.at[0], recv1_sem.at[0])
    lax.fori_loop(0, 8, inner(1), 0)
    exchange(send1.at[1], recv1.at[1], send1_sem.at[1], recv1_sem.at[1])

    for copy in tables:
        copy.wait()
    me_lane = iota((FREQS, 128), 1) == me
    col_cos = jnp.sum(jnp.where(me_lane, v_col[0], 0.0), axis=1, keepdims=True)
    col_sin = jnp.sum(jnp.where(me_lane, v_col[1], 0.0), axis=1, keepdims=True)
    row_cos = v_row[0, pl.ds(me, 1), :]
    row_sin = v_row[1, pl.ds(me, 1), :]
    turn[0] = col_cos * row_cos - col_sin * row_sin
    turn[1] = col_cos * row_sin + col_sin * row_cos
    lane1 = iota((1, 128), 1)
    lane8, sub8 = iota((8, 128), 1), iota((8, 128), 0)

    def transform(trial):
        d_high, d_low = split(recv1[trial])
        spectrum[...] = product(v_first_high[...], v_first_low[...], d_high, d_low)
        real, imaginary = spectrum[0:FREQS, :], spectrum[FREQS : 2 * FREQS, :]
        mid_cos, mid_sin = v_mid[0], v_mid[1]
        turned = jnp.concatenate(
            [real * mid_cos - imaginary * mid_sin, real * mid_sin + imaginary * mid_cos], 1
        )
        t_high, t_low = split(turned)
        s_high = v_second_high[...]
        result = dot(t_high, s_high) + dot(t_low, s_high) + dot(t_high, v_second_low[...])
        real, imaginary = result[:, 0:128], result[:, 128:256]
        turn_cos, turn_sin = turn[0], turn[1]
        parts = (
            real * turn_cos - imaginary * turn_sin,
            real * turn_sin + imaginary * turn_cos,
        )
        middle = pltpu.roll(real[0:1], 64, 1)
        for c in range(2):
            for i in range(4):
                send2[trial, pl.ds(2 * i + c, 64, stride=8), :] = parts[c][64 * i : 64 * i + 64]
            packed = jnp.where(lane1 < 64, parts[c][0:1], pltpu.roll(parts[c][256:257], 64, 1))
            if c == 1:
                packed = jnp.where(lane1 == 0, middle, packed)
            send2[trial, c : c + 1, :] = packed

    def finish(trial):
        r_high, r_low = split(recv2[trial])
        final = product(v_last_high[...], v_last_low[...], r_high, r_low)
        power = powers.at[trial]
        power[...] = final[0:64] ** 2 + final[64:128] ** 2
        special = final[128:144] ** 2 + final[144:160] ** 2

        @pl.when(me == 0)
        def _():
            for sign in range(2):
                where = pl.ds(4 * sign, 8, stride=8)
                power[where, :] = jnp.where(
                    lane8 == 0, special[8 * sign : 8 * sign + 8], power[where, :]
                )
            for p in range(8):
                x = power[8 * p : 8 * p + 8, :]
                one = lanes_at(
                    pltpu.roll(x, 7, 0), jnp.where(sub8 == 7, lane8 + 64, 127 - lane8) & 127
                )
                two = lanes_at(
                    jnp.where(sub8 == 0, pltpu.roll(x, 4, 0), pltpu.roll(x, 3, 0)),
                    jnp.where(sub8 == 0, (128 - lane8) & 63, (191 - lane8) & 127),
                )
                head = jnp.where((sub8 == 0) & (lane8 >= 64), two, x)
                tail = jnp.where((sub8 == 7) & (lane8 >= 64), two, one)
                power[8 * p : 8 * p + 8, :] = jnp.where(sub8 < 4, head, tail)

        @pl.when(me != 0)
        def _():
            for p in range(8):
                x = power[8 * p : 8 * p + 8, :]
                power[8 * p : 8 * p + 8, :] = jnp.where(sub8 < 4, x, lanes_at(x, 127 - lane8))

        for n in range(8):
            rows_a[trial, 8 * n : 8 * n + 8, :] = power[pl.ds(n, 8, stride=8), :]

    def residue(sign):
        return me if sign == 0 else (SLOTS - me) & (SLOTS - 1)

    class_of = jnp.where(sub8 < 4, me, (SLOTS - me) & (SLOTS - 1)) + 64 * jnp.where(
        sub8 < 4, sub8, 11 - sub8
    )

    def select(trial, m, odd, shift, half):
        k1 = (INVERSE[odd] * (class_of >> shift)) & ((FIRST >> shift) - 1)
        index = ((m * k1) >> 9) + odd * (128 * half + lane8)
        total = jnp.zeros((8, 128), f32)
        for p in range(odd * half, odd * half + odd):
            total = jnp.where(
                (index >> 7) == p,
                lanes_at(powers[trial, 8 * p : 8 * p + 8, :], index & 127),
                total,
            )
        return total

    started = []

    def share(trial):
        power, by_row, term = powers.at[trial], rows_a.at[trial], terms.at[trial]
        number = [0]

        def give(source, start, m, sign, rows, to, condition):
            base = BASES[m] + (0 if m == 8 else rows * sign)
            from_ref = source.at[pl.ds(start, rows)]
            to_ref = received.at[trial, pl.ds(base, rows)]
            copy = pltpu.make_async_remote_copy(
                src_ref=from_ref, dst_ref=to_ref,
                send_sem=term_send.at[trial, number[0]], recv_sem=term_recv.at[trial],
                device_id={"fft": to}, device_id_type=mesh_id,
            )
            number[0] += 1
            away = condition & (to != me)

            @pl.when(away)
            def _():
                copy.start()

            @pl.when(condition & (to == me))
            def _():
                pltpu.make_async_copy(from_ref, to_ref, term_recv.at[trial]).start()

            started.append((copy, away))

        always, even = me >= 0, (me & 1) == 0
        for sign in range(2):
            rest = residue(sign)
            give(power, 0, 1, sign, 8, rest, always)
            for v in range(2):
                give(power, 0, 2, sign, 16, ((rest >> 1) + 32 * v) & 63, even)
            for i in range(4):
                place = i if sign == 0 else 7 - i
                at = 32 * sign + 8 * i
                give(by_row, at, 4, sign, 8, ((rest >> 2) + 16 * place) & 63, (me & 3) == 0)
                give(by_row, at, 8, sign, 8, ((rest >> 3) + 8 * place) & 63, (me & 7) == 0)
        for n, m in enumerate((3, 5, 7)):
            term[8 * n : 8 * n + 8, :] = select(trial, m, m, 0, 0)
            for sign in range(2):
                give(term, 8 * n, m, sign, 8, (INVERSE[m] * residue(sign)) & 63, always)
        for half in range(2):
            term[24 + 8 * half : 32 + 8 * half, :] = select(trial, 6, 3, 1, half)
        for sign in range(2):
            for v in range(2):
                to = (INVERSE[3] * ((residue(sign) >> 1) + 32 * v)) & 63
                give(term, 24, 6, sign, 16, to, even)

    def source_row(m, v, rows):
        place = (((m * me) >> 6) + m * v) & 7
        sign = place >> 2
        slot = jnp.where(sign == 1, 7 - place, place)
        return BASES[m] + (rows + 4) * sign + slot

    def collect(trial):
        def row_at(index):
            return received[trial, pl.ds(index, 1), :]

        total = received[trial, pl.ds(BASES[8], 8), :]
        for v in range(2):
            base = BASES[4] + 8 * v
            values = jnp.broadcast_to(row_at(base), (8, 128))
            for p in range(1, 4):
                values = jnp.where((sub8 >> 1) == p, row_at(base + p), values)
            values = lanes_at(values, 64 * (sub8 & 1) + (lane8 >> 1))
            total = total + jnp.where((lane8 & 1) == v, values, 0.0)
        for v in range(4):
            at2, at6 = source_row(2, v, 16), source_row(6, v, 16)
            low = row_at(at2) + row_at(at6)
            high = row_at(at2 + 8) + row_at(at6 + 8)
            values = jnp.where((sub8 >> 2) == 0, low, high)
            values = lanes_at(values, 32 * (sub8 & 3) + (lane8 >> 2))
            total = total + jnp.where((lane8 & 3) == v, values, 0.0)
        for v in range(8):
            values = row_at(source_row(1, v, 8))
            for m in (3, 5, 7):
                values = values + row_at(source_row(m, v, 8))
            values = lanes_at(jnp.broadcast_to(values, (8, 128)), 16 * sub8 + (lane8 >> 3))
            total = total + jnp.where((lane8 & 7) == v, values, 0.0)
        out[trial] = total * (0.125 / LENGTH)

    for trial in range(2):
        arrived(recv1.at[trial], recv1_sem.at[trial])
        transform(trial)
        exchange(send2.at[trial], recv2.at[trial], send2_sem.at[trial], recv2_sem.at[trial])
    for trial in range(2):
        arrived(recv2.at[trial], recv2_sem.at[trial])
        finish(trial)
        share(trial)
    for trial in range(2):
        arrived(received.at[trial], term_recv.at[trial])
        collect(trial)

    @pl.when(me < SLOTS - 1)
    def _():
        to_next.wait_send()

    @pl.when(me > 0)
    def _():
        to_last.wait_send()

    for trial in range(2):
        sent(send1.at[trial], send1_sem.at[trial])
        sent(send2.at[trial], send2_sem.at[trial])
    for copy, away in started:

        @pl.when(away)
        def _(copy=copy):
            copy.wait_send()


def on_device(series, filters, delays, phases):
    tables = [jnp.asarray(table) for table in make_tables()]
    whole = pl.BlockSpec(memory_space=pltpu.VMEM)
    anywhere = pl.BlockSpec(memory_space=pl.ANY)
    f32 = jnp.float32
    out = pl.pallas_call(
        kernel,
        out_shape=jax.ShapeDtypeStruct((2, 8, 128), f32),
        in_specs=[anywhere, whole, whole, whole] + [anywhere] * len(tables),
        out_specs=whole,
        scratch_shapes=[
            pltpu.VMEM((528, 128), f32),
            pltpu.VMEM((32, 256), f32),
            pltpu.VMEM((8, 256, 128), jnp.bfloat16),
            pltpu.VMEM((8, 256, 128), jnp.bfloat16),
            pltpu.VMEM((2, 512, 128), f32),
            pltpu.VMEM((2, 512, 128), f32),
            pltpu.VMEM((2, 512, 128), f32),
            pltpu.VMEM((2, 512, 128), f32),
            pltpu.VMEM((2 * FREQS, 128), f32),
            pltpu.VMEM((2, FREQS, 128), f32),
            pltpu.VMEM((2, 64, 128), f32),
            pltpu.VMEM((2, 64, 128), f32),
            pltpu.VMEM((2, 40, 128), f32),
            pltpu.VMEM((2, TERM_ROWS, 128), f32),
        ]
        + [pltpu.VMEM(table.shape, table.dtype) for table in tables]
        + [
            pltpu.SemaphoreType.DMA((len(tables),)),
            pltpu.SemaphoreType.DMA,
            pltpu.SemaphoreType.DMA((2,)),
            pltpu.SemaphoreType.DMA((2,)),
            pltpu.SemaphoreType.DMA((2,)),
            pltpu.SemaphoreType.DMA((2,)),
            pltpu.SemaphoreType.DMA((2,)),
            pltpu.SemaphoreType.DMA((2,)),
            pltpu.SemaphoreType.DMA((2, 32)),
            pltpu.SemaphoreType.DMA((2,)),
        ],
        compiler_params=pltpu.CompilerParams(
            collective_id=0, has_side_effects=True
        ),
    )(series.reshape(512, 128), delays, phases, filters.T, *tables)
    return out.reshape(2, 1, 1024)


def solution(mesh):
    return jax.shard_map(
        on_device,
        mesh=mesh,
        in_specs=(P(("dm", "fft")), P(), P(None, "fft"), P(None, "fft")),
        out_specs=P("dm", "fft", None),
        check_vma=False,
    )
```

time: 69.8 us -> 52.1 us (0.75)
  local copies, waits for them, and re-layouts: 11.6 us -> 1.3 us
  Pallas kernels: 57.7 us -> 50.6 us
    unnamed x26 -> x1, local copies, waits for them, and re-layouts: 11.6 us -> 1.3 us
    pallas_call x1, Pallas kernels: 57.7 us -> 50.6 us  [on_device(): pl.pallas_call(kernel, out_shape=jax.ShapeDtypeStruct((2, 8, 128), f32),...]
where the time goes in v2:
time: 52.1 us; the launch traced here: 51.9 us
  Pallas kernels  50.6 us (97%)
  local copies, waits for them, and re-layouts  1.3 us (2%)
    pallas_call x1, Pallas kernels, on_device(): pl.pallas_call(kernel, out_shape=jax.ShapeDtypeStruct((2, 8, 128), f32),...  50.6 us
    unnamed x1, local copies, waits for them, and re-layouts  1.3 us

profile of v2, /device:TPU:1, one launch (start us, length us, event | category | flops | bytes accessed | tf_op | source)
XLA Modules:
  0.0 51.9 jit_solution(12616096465770602667)
XLA Ops:
  0.0 50.6 %shard_map.127 = f32[2,8,128]{2,1,0:T(8,128)} custom-call(f32[512,128]{1,0:T(8,128)} %bitcast.3, s32[2,16]{1,0:T(2,128)} %delays.1, s32[2,16]{1,0:T(2,128)} %phases.1, f32[16,32]{1,0:T(8,128)} %bitcast.5, bf16[544,512]{1,0:T(8,128)(2,1)} %constant.18.clone.first_high, bf16[544,512]{1,0:T(8,128)(2,1)} %constant.19.clone.first_low, ...), custom_call_target="tpu_custom_call" | custom-call | tf_op jit(solution)/shard_map/pallas_call | solution.py:463
  50.6 1.3 %copy.16 = f32[2,1,1024]{2,1,0:T(1,128)} copy(f32[2,1,1024]{2,1,0:T(1,128)} %bitcast.4) | data formatting | bytes 16384

commit v3 on v2

--- a/solution.py
+++ b/solution.py
@@ -91,11 +91,11 @@
     series, delays, phases, filters,
     first_high, first_low, second_high, second_low, last_high, last_low, mid, col, row,
     out,
-    ext, responses, windows_high, windows_low, send1, recv1, send2, recv2, spectrum, turn,
+    v_delays, v_phases, v_filters, ext, halos, fixes, fixed, responses, windows_high, windows_low, send1, recv1, send2, recv2, spectrum, turn,
     powers, rows_a, terms, received,
     v_first_high, v_first_low, v_second_high, v_second_low, v_last_high, v_last_low,
     v_mid, v_col, v_row,
-    table_sem, series_sem, halo_send, halo_recv,
+    small_sem, table_sem, series_sem, halo_send, halo_recv, fix_sem,
     send1_sem, recv1_sem, send2_sem, recv2_sem, term_send, term_recv,
 ):
     me = lax.axis_index("fft")
@@ -104,14 +104,36 @@
 
     barrier = pltpu.get_barrier_semaphore()
 
-    def greet(step, carry):
-        pl.semaphore_signal(
-            barrier, inc=1, device_id={"fft": (me + step) & (SLOTS - 1)}, device_id_type=mesh_id
+    def partners(act):
+        def partner(dz, dy, dc):
+            y, z = ((me >> 4) + dy) & 3, ((me >> 1) + dz) & 7
+            act((y << 4) + (z << 1) + ((me & 1) ^ dc))
+
+        def ring(step, carry):
+            side = jnp.where((step & 1) == 1, (step + 1) >> 1, -(step >> 1))
+            for dy in (2, 1, 3, 0):
+                for dc in range(2):
+                    partner(4 + side, dy, dc)
+            return carry
+
+        lax.fori_loop(0, 7, ring, 0)
+        for dy in (2, 1, 3, 0):
+            for dc in range(2):
+                if dy or dc:
+                    partner(0, dy, dc)
+
+    def greet(to):
+        pl.semaphore_signal(barrier, inc=1, device_id={"fft": to}, device_id_type=mesh_id)
+
+    small = [
+        pltpu.make_async_copy(source, target, small_sem.at[n])
+        for n, (source, target) in enumerate(
+            ((delays, v_delays), (phases, v_phases), (filters, v_filters))
         )
-        return carry
-
-    lax.fori_loop(1, SLOTS, greet, 0)
-
+    ]
+    for copy in small:
+        copy.start()
+    partners(greet)
     own_series = pltpu.make_async_copy(series, ext.at[pl.ds(8, 512)], series_sem)
     own_series.start()
     tables = [
@@ -128,14 +150,16 @@
     for copy in tables:
         copy.start()
 
+    for copy in small:
+        copy.wait()
     line = iota((32, 16), 0)
     own = iota((32, 16), 1) == 2 * (line >> 2) + (line & 1)
     second_trial = ((line >> 1) & 1) == 1
-    delay = column_of(delays[...].astype(f32), own, second_trial)
-    phase = column_of(phases[...].astype(f32), own, second_trial)
+    delay = column_of(v_delays[...].astype(f32), own, second_trial)
+    phase = column_of(v_phases[...].astype(f32), own, second_trial)
     branch = (iota((32, PHASES), 1).astype(f32) == phase).astype(f32)
     taps = lax.dot_general(
-        branch, filters[...], (((1,), (1,)), ((), ())),
+        branch, v_filters[...], (((1,), (1,)), ((), ())),
         precision=lax.Precision.HIGHEST, preferred_element_type=f32,
     )
     position = iota((32, 256), 1).astype(f32) - (delay + 56.0)
@@ -144,30 +168,11 @@
         response = jnp.where(position == float(tap), taps[:, tap : tap + 1], response)
     responses[...] = response
 
-    pl.semaphore_wait(barrier, SLOTS - 1)
-    to_next = pltpu.make_async_remote_copy(
-        src_ref=series.at[pl.ds(504, 8)], dst_ref=ext.at[pl.ds(0, 8)],
-        send_sem=halo_send.at[0], recv_sem=halo_recv.at[0],
-        device_id={"fft": (me + 1) & (SLOTS - 1)}, device_id_type=mesh_id,
-    )
-    to_last = pltpu.make_async_remote_copy(
-        src_ref=series.at[pl.ds(0, 8)], dst_ref=ext.at[pl.ds(520, 8)],
-        send_sem=halo_send.at[1], recv_sem=halo_recv.at[1],
-        device_id={"fft": (me + SLOTS - 1) & (SLOTS - 1)}, device_id_type=mesh_id,
-    )
-
-    @pl.when(me < SLOTS - 1)
-    def _():
-        to_next.start()
-
-    @pl.when(me > 0)
-    def _():
-        to_last.start()
-
     own_series.wait()
+    ext[0:8, :] = jnp.zeros((8, 128), f32)
+    ext[520:528, :] = jnp.zeros((8, 128), f32)
 
     lane64 = iota((64, 128), 1)
-    quarter = lane64 >> 5
 
     def resample(trial, rg):
         if trial == 0:
@@ -177,7 +182,7 @@
             left = pltpu.roll(jnp.where(lane64 < 64, here, before), 64, 1)
             right = pltpu.roll(jnp.where(lane64 < 64, after, here), 64, 1)
             window = jnp.concatenate(
-                [jnp.concatenate([left, left], 0).T, jnp.concatenate([right, right], 0).T], 0
+                [jnp.concatenate([left, here], 0).T, jnp.concatenate([right, after], 0).T], 0
             )
             w_high, w_low = split(window)
             windows_high[rg], windows_low[rg] = w_high, w_low
@@ -187,66 +192,78 @@
         for rr in range(2):
             line = responses[pl.ds(4 * rg + 2 * trial + rr, 1), :]
             bands.append(
-                pltpu.roll(jnp.broadcast_to(line, (128, 256)), 0, 1, stride=1, stride_axis=0)
+                pltpu.roll(jnp.broadcast_to(line, (64, 256)), 0, 1, stride=1, stride_axis=0)
             )
         b_high, b_low = split(jnp.concatenate(bands, 0))
         both = product(b_high, b_low, w_high, w_low)
-        total = jnp.where((quarter & 1) == 0, both[0:64], both[128:192])
-        later = jnp.where((quarter & 1) == 0, both[64:128], both[192:256])
-        send1[trial, pl.ds(rg, 64, stride=8), :] = jnp.where(quarter < 2, total, later)
-
-    def exchange(source, target, send_sem, recv_sem):
-        mine = pl.ds(pl.multiple_of(8 * me, 8), 8)
-
-        def send(step, carry):
-            to = (me + step) & (SLOTS - 1)
+        return jnp.where((lane64 & 32) == 0, both[0:64], both[64:128])
+
+    def exchange(source, target, send_sem, recv_sem, rows=8):
+        mine = pl.ds(pl.multiple_of(8 * me, 8), rows)
+
+        def send(to):
             pltpu.make_async_remote_copy(
-                src_ref=source.at[pl.ds(pl.multiple_of(8 * to, 8), 8)],
+                src_ref=source.at[pl.ds(pl.multiple_of(8 * to, 8), rows)],
                 dst_ref=target.at[mine],
                 send_sem=send_sem, recv_sem=recv_sem,
                 device_id={"fft": to}, device_id_type=mesh_id,
             ).start()
-            return carry
-
-        lax.fori_loop(1, SLOTS, send, 0)
+
+        partners(send)
         pltpu.make_async_copy(source.at[mine], target.at[mine], recv_sem).start()
 
     def arrived(target, sem):
         pltpu.make_async_copy(target, target, sem).wait()
 
-    def sent(source, sem):
-        part = source.at[pl.ds(0, 8 * (SLOTS - 1))]
+    def sent(source, sem, rows=8):
+        part = source.at[pl.ds(0, rows * (SLOTS - 1))]
         pltpu.make_async_copy(part, part, sem).wait()
 
     def inner(trial):
         def body(rg, carry):
-            resample(trial, rg)
+            send1[trial, pl.ds(rg, 64, stride=8), :] = resample(trial, rg)
             return carry
 
         return body
 
-    lax.fori_loop(1, 7, inner(0), 0)
+    lax.fori_loop(0, 8, inner(0), 0)
+    lax.fori_loop(1, 7, inner(1), 0)
+    pl.semaphore_wait(barrier, SLOTS - 1)
+    to_next = pltpu.make_async_remote_copy(
+        src_ref=series.at[pl.ds(504, 8)], dst_ref=halos.at[0],
+        send_sem=halo_send.at[0], recv_sem=halo_recv.at[0],
+        device_id={"fft": (me + 1) & (SLOTS - 1)}, device_id_type=mesh_id,
+    )
+    to_last = pltpu.make_async_remote_copy(
+        src_ref=series.at[pl.ds(0, 8)], dst_ref=halos.at[1],
+        send_sem=halo_send.at[1], recv_sem=halo_recv.at[1],
+        device_id={"fft": (me + SLOTS - 1) & (SLOTS - 1)}, device_id_type=mesh_id,
+    )
+
+    @pl.when(me < SLOTS - 1)
+    def _():
+        to_next.start()
+
+    @pl.when(me > 0)
+    def _():
+        to_last.start()
+
+    exchange(send1.at[0], recv1.at[0], send1_sem.at[0], recv1_sem.at[0])
 
     @pl.when(me > 0)
     def _():
         to_next.wait_recv()
-
-    @pl.when(me == 0)
-    def _():
-        ext[0:8, :] = jnp.zeros((8, 128), f32)
+        ext[0:8, :] = halos[0]
 
     @pl.when(me < SLOTS - 1)
     def _():
         to_last.wait_recv()
-
-    @pl.when(me == SLOTS - 1)
-    def _():
-        ext[520:528, :] = jnp.zeros((8, 128), f32)
-
-    resample(0, 0)
-    resample(0, 7)
-    exchange(send1.at[0], recv1.at[0], send1_sem.at[0], recv1_sem.at[0])
-    lax.fori_loop(0, 8, inner(1), 0)
+        ext[520:528, :] = halos[1]
+
+    fixes[pl.ds(0, 64, stride=8), :] = jnp.where(lane64 == 0, resample(0, 0), resample(0, 7))
+    exchange(fixes, fixed, fix_sem.at[0], fix_sem.at[1], 1)
+    for rg in (0, 7):
+        send1[1, pl.ds(rg, 64, stride=8), :] = resample(1, rg)
     exchange(send1.at[1], recv1.at[1], send1_sem.at[1], recv1_sem.at[1])
 
     for copy in tables:
@@ -427,15 +444,20 @@
 
     for trial in range(2):
         arrived(recv1.at[trial], recv1_sem.at[trial])
+        if trial == 0:
+            arrived(fixed.at[pl.ds(0, SLOTS)], fix_sem.at[1])
+            right = fixed[pl.ds(0, 64, stride=8), :]
+            for rg, at in ((0, 0), (7, 127)):
+                where = pl.ds(rg, 64, stride=8)
+                recv1[0, where, :] = jnp.where(lane64 == at, right, recv1[0, where, :])
         transform(trial)
         exchange(send2.at[trial], recv2.at[trial], send2_sem.at[trial], recv2_sem.at[trial])
     for trial in range(2):
         arrived(recv2.at[trial], recv2_sem.at[trial])
         finish(trial)
         share(trial)
-    for trial in range(2):
-        arrived(received.at[trial], term_recv.at[trial])
-        collect(trial)
+    arrived(received.at[0], term_recv.at[0])
+    collect(0)
 
     @pl.when(me < SLOTS - 1)
     def _():
@@ -445,6 +467,7 @@
     def _():
         to_last.wait_send()
 
+    sent(fixes, fix_sem.at[0], 1)
     for trial in range(2):
         sent(send1.at[trial], send1_sem.at[trial])
         sent(send2.at[trial], send2_sem.at[trial])
@@ -453,6 +476,9 @@
         @pl.when(away)
         def _(copy=copy):
             copy.wait_send()
+
+    arrived(received.at[1], term_recv.at[1])
+    collect(1)
 
 
 def on_device(series, filters, delays, phases):
@@ -463,10 +489,16 @@
     out = pl.pallas_call(
         kernel,
         out_shape=jax.ShapeDtypeStruct((2, 8, 128), f32),
-        in_specs=[anywhere, whole, whole, whole] + [anywhere] * len(tables),
+        in_specs=[anywhere] * (4 + len(tables)),
         out_specs=whole,
         scratch_shapes=[
+            pltpu.VMEM((2, 16), jnp.int32),
+            pltpu.VMEM((2, 16), jnp.int32),
+            pltpu.VMEM((TAPS, PHASES), f32),
             pltpu.VMEM((528, 128), f32),
+            pltpu.VMEM((2, 8, 128), f32),
+            pltpu.VMEM((512, 128), f32),
+            pltpu.VMEM((512, 128), f32),
             pltpu.VMEM((32, 256), f32),
             pltpu.VMEM((8, 256, 128), jnp.bfloat16),
             pltpu.VMEM((8, 256, 128), jnp.bfloat16),
@@ -483,8 +515,10 @@
         ]
         + [pltpu.VMEM(table.shape, table.dtype) for table in tables]
         + [
+            pltpu.SemaphoreType.DMA((3,)),
             pltpu.SemaphoreType.DMA((len(tables),)),
             pltpu.SemaphoreType.DMA,
+            pltpu.SemaphoreType.DMA((2,)),
             pltpu.SemaphoreType.DMA((2,)),
             pltpu.SemaphoreType.DMA((2,)),
             pltpu.SemaphoreType.DMA((2,)),

time: 52.1 us -> 49.6 us (0.952)
  Pallas kernels: 50.6 us -> 48.1 us
    pallas_call x1, Pallas kernels: 50.6 us -> 48.1 us  [on_device(): pl.pallas_call(kernel, out_shape=jax.ShapeDtypeStruct((2, 8, 128), f32),...]
where the time goes in v3:
time: 49.6 us; the launch traced here: 49.4 us
  Pallas kernels  48.1 us (97%)
  local copies, waits for them, and re-layouts  1.3 us (3%)
    pallas_call x1, Pallas kernels, on_device(): pl.pallas_call(kernel, out_shape=jax.ShapeDtypeStruct((2, 8, 128), f32),...  48.1 us
    unnamed x1, local copies, waits for them, and re-layouts  1.3 us

profile of v3, /device:TPU:1, one launch (start us, length us, event | category | flops | bytes accessed | tf_op | source)
XLA Modules:
  0.0 49.4 jit_solution(9978134746406245473)
XLA Ops:
  0.0 48.1 %shard_map.127 = f32[2,8,128]{2,1,0:T(8,128)} custom-call(f32[512,128]{1,0:T(8,128)} %bitcast.3, s32[2,16]{1,0:T(2,128)} %delays.1, s32[2,16]{1,0:T(2,128)} %phases.1, f32[16,32]{1,0:T(8,128)} %bitcast.5, bf16[544,512]{1,0:T(8,128)(2,1)} %constant.18.clone.first_high, bf16[544,512]{1,0:T(8,128)(2,1)} %constant.19.clone.first_low, ...), custom_call_target="tpu_custom_call" | custom-call | tf_op jit(solution)/shard_map/pallas_call | solution.py:489
  48.1 1.3 %copy.16 = f32[2,1,1024]{2,1,0:T(1,128)} copy(f32[2,1,1024]{2,1,0:T(1,128)} %bitcast.4) | data formatting | bytes 16384

commit v4 on v3

--- a/solution.py
+++ b/solution.py
@@ -17,6 +17,10 @@
 INVERSE = {1: 1, 3: 171, 5: 205, 7: 439}
 BASES = {1: 0, 3: 16, 5: 32, 7: 48, 2: 64, 6: 96, 4: 128, 8: 144}
 TERM_ROWS = 152
+PAIRS = (
+    6, 16, 3, 24, 18, 22, 2, 15, 5, 4, 21, 12, 28, 17, 31, 8,
+    7, 9, 20, 19, 25, 11, 13, 26, 0, 30, 14, 10, 23, 29, 27, 1,
+)
 
 
 def split_table(table):
@@ -82,6 +86,17 @@
     return lax.broadcasted_iota(jnp.int32, shape, axis)
 
 
+def class_at(device):
+    words = [sum(PAIRS[4 * n + b] << (8 * b) for b in range(4)) for n in range(8)]
+    chip = device >> 1
+    word = jnp.int32(words[0])
+    for n in range(1, 8):
+        word = jnp.where((chip >> 2) == n, jnp.int32(words[n]), word)
+    pair = (word >> ((chip & 3) << 3)) & 31
+    other = jnp.where(pair == 0, SLOTS // 2, SLOTS - pair)
+    return jnp.where((device & 1) == 0, pair, other)
+
+
 def column_of(values, own, second_trial):
     chosen = jnp.where(second_trial, values[1:2, :], values[0:1, :])
     return jnp.sum(jnp.where(own, chosen, 0.0), axis=1, keepdims=True)
@@ -99,6 +114,7 @@
     send1_sem, recv1_sem, send2_sem, recv2_sem, term_send, term_recv,
 ):
     me = lax.axis_index("fft")
+    cls = class_at(me)
     f32 = jnp.float32
     mesh_id = pl.DeviceIdType.MESH
 
@@ -109,18 +125,11 @@
             y, z = ((me >> 4) + dy) & 3, ((me >> 1) + dz) & 7
             act((y << 4) + (z << 1) + ((me & 1) ^ dc))
 
-        def ring(step, carry):
-            side = jnp.where((step & 1) == 1, (step + 1) >> 1, -(step >> 1))
-            for dy in (2, 1, 3, 0):
-                for dc in range(2):
-                    partner(4 + side, dy, dc)
-            return carry
-
-        lax.fori_loop(0, 7, ring, 0)
         for dy in (2, 1, 3, 0):
             for dc in range(2):
-                if dy or dc:
-                    partner(0, dy, dc)
+                for dz in (4, 3, 5, 2, 6, 1, 7, 0):
+                    if dz or dy or dc:
+                        partner(dz, dy, dc)
 
     def greet(to):
         pl.semaphore_signal(barrier, inc=1, device_id={"fft": to}, device_id_type=mesh_id)
@@ -198,19 +207,21 @@
         both = product(b_high, b_low, w_high, w_low)
         return jnp.where((lane64 & 32) == 0, both[0:64], both[64:128])
 
-    def exchange(source, target, send_sem, recv_sem, rows=8):
+    def exchange(source, target, send_sem, recv_sem, rows=8, block_of=lambda device: device):
         mine = pl.ds(pl.multiple_of(8 * me, 8), rows)
+
+        def block(device):
+            return source.at[pl.ds(pl.multiple_of(8 * block_of(device), 8), rows)]
 
         def send(to):
             pltpu.make_async_remote_copy(
-                src_ref=source.at[pl.ds(pl.multiple_of(8 * to, 8), rows)],
-                dst_ref=target.at[mine],
+                src_ref=block(to), dst_ref=target.at[mine],
                 send_sem=send_sem, recv_sem=recv_sem,
                 device_id={"fft": to}, device_id_type=mesh_id,
             ).start()
 
         partners(send)
-        pltpu.make_async_copy(source.at[mine], target.at[mine], recv_sem).start()
+        pltpu.make_async_copy(block(me), target.at[mine], recv_sem).start()
 
     def arrived(target, sem):
         pltpu.make_async_copy(target, target, sem).wait()
@@ -311,7 +322,7 @@
         power[...] = final[0:64] ** 2 + final[64:128] ** 2
         special = final[128:144] ** 2 + final[144:160] ** 2
 
-        @pl.when(me == 0)
+        @pl.when(cls == 0)
         def _():
             for sign in range(2):
                 where = pl.ds(4 * sign, 8, stride=8)
@@ -331,7 +342,7 @@
                 tail = jnp.where((sub8 == 7) & (lane8 >= 64), two, one)
                 power[8 * p : 8 * p + 8, :] = jnp.where(sub8 < 4, head, tail)
 
-        @pl.when(me != 0)
+        @pl.when(cls != 0)
         def _():
             for p in range(8):
                 x = power[8 * p : 8 * p + 8, :]
@@ -341,9 +352,9 @@
             rows_a[trial, 8 * n : 8 * n + 8, :] = power[pl.ds(n, 8, stride=8), :]
 
     def residue(sign):
-        return me if sign == 0 else (SLOTS - me) & (SLOTS - 1)
-
-    class_of = jnp.where(sub8 < 4, me, (SLOTS - me) & (SLOTS - 1)) + 64 * jnp.where(
+        return cls if sign == 0 else (SLOTS - cls) & (SLOTS - 1)
+
+    class_of = jnp.where(sub8 < 4, cls, (SLOTS - cls) & (SLOTS - 1)) + 64 * jnp.where(
         sub8 < 4, sub8, 11 - sub8
     )
 
@@ -387,7 +398,7 @@
 
             started.append((copy, away))
 
-        always, even = me >= 0, (me & 1) == 0
+        always, even = me >= 0, (cls & 1) == 0
         for sign in range(2):
             rest = residue(sign)
             give(power, 0, 1, sign, 8, rest, always)
@@ -396,8 +407,8 @@
             for i in range(4):
                 place = i if sign == 0 else 7 - i
                 at = 32 * sign + 8 * i
-                give(by_row, at, 4, sign, 8, ((rest >> 2) + 16 * place) & 63, (me & 3) == 0)
-                give(by_row, at, 8, sign, 8, ((rest >> 3) + 8 * place) & 63, (me & 7) == 0)
+                give(by_row, at, 4, sign, 8, ((rest >> 2) + 16 * place) & 63, (cls & 3) == 0)
+                give(by_row, at, 8, sign, 8, ((rest >> 3) + 8 * place) & 63, (cls & 7) == 0)
         for n, m in enumerate((3, 5, 7)):
             term[8 * n : 8 * n + 8, :] = select(trial, m, m, 0, 0)
             for sign in range(2):
@@ -451,7 +462,10 @@
                 where = pl.ds(rg, 64, stride=8)
                 recv1[0, where, :] = jnp.where(lane64 == at, right, recv1[0, where, :])
         transform(trial)
-        exchange(send2.at[trial], recv2.at[trial], send2_sem.at[trial], recv2_sem.at[trial])
+        exchange(
+            send2.at[trial], recv2.at[trial], send2_sem.at[trial], recv2_sem.at[trial],
+            block_of=class_at,
+        )
     for trial in range(2):
         arrived(recv2.at[trial], recv2_sem.at[trial])
         finish(trial)

time: 49.6 us -> 47.4 us (0.956)
  Pallas kernels: 48.1 us -> 45.9 us
    pallas_call x1, Pallas kernels: 48.1 us -> 45.9 us  [on_device(): pl.pallas_call(kernel, out_shape=jax.ShapeDtypeStruct((2, 8, 128), f32),...]
where the time goes in v4:
time: 47.4 us; the launch traced here: 47.2 us
  Pallas kernels  45.9 us (97%)
  local copies, waits for them, and re-layouts  1.3 us (3%)
    pallas_call x1, Pallas kernels, on_device(): pl.pallas_call(kernel, out_shape=jax.ShapeDtypeStruct((2, 8, 128), f32),...  45.9 us
    unnamed x1, local copies, waits for them, and re-layouts  1.3 us

profile of v4, /device:TPU:1, one launch (start us, length us, event | category | flops | bytes accessed | tf_op | source)
XLA Modules:
  0.0 47.2 jit_solution(7289472360984979050)
XLA Ops:
  0.0 45.9 %shard_map.127 = f32[2,8,128]{2,1,0:T(8,128)} custom-call(f32[512,128]{1,0:T(8,128)} %bitcast.3, s32[2,16]{1,0:T(2,128)} %delays.1, s32[2,16]{1,0:T(2,128)} %phases.1, f32[16,32]{1,0:T(8,128)} %bitcast.5, bf16[544,512]{1,0:T(8,128)(2,1)} %constant.18.clone.first_high, bf16[544,512]{1,0:T(8,128)(2,1)} %constant.19.clone.first_low, ...), custom_call_target="tpu_custom_call" | custom-call | tf_op jit(solution)/shard_map/pallas_call | solution.py:503
  45.9 1.3 %copy.16 = f32[2,1,1024]{2,1,0:T(1,128)} copy(f32[2,1,1024]{2,1,0:T(1,128)} %bitcast.4) | data formatting | bytes 16384

commit v5 on v4

--- a/solution.py
+++ b/solution.py
@@ -120,16 +120,36 @@
 
     barrier = pltpu.get_barrier_semaphore()
 
-    def partners(act):
-        def partner(dz, dy, dc):
-            y, z = ((me >> 4) + dy) & 3, ((me >> 1) + dz) & 7
-            act((y << 4) + (z << 1) + ((me & 1) ^ dc))
-
+    def partner(act, dz, dy, dc):
+        y, z = ((me >> 4) + dy) & 3, ((me >> 1) + dz) & 7
+        act((y << 4) + (z << 1) + ((me & 1) ^ dc))
+
+    def same_z(act):
         for dy in (2, 1, 3, 0):
             for dc in range(2):
-                for dz in (4, 3, 5, 2, 6, 1, 7, 0):
-                    if dz or dy or dc:
-                        partner(dz, dy, dc)
+                if dy or dc:
+                    partner(act, 0, dy, dc)
+
+    def partners(act):
+        def block(step, carry):
+            dy = (0x36 >> (step & 6)) & 3
+            for dz in (3, 5, 4, 2, 6, 1, 7):
+                partner(act, dz, dy, step & 1)
+            return carry
+
+        lax.fori_loop(0, 8, block, 0)
+        same_z(act)
+
+    def far_first(act):
+        def ring(step, carry):
+            dz = (0x7162534 >> (4 * step)) & 7
+            for dy in (2, 1, 3, 0):
+                for dc in range(2):
+                    partner(act, dz, dy, dc)
+            return carry
+
+        lax.fori_loop(0, 7, ring, 0)
+        same_z(act)
 
     def greet(to):
         pl.semaphore_signal(barrier, inc=1, device_id={"fft": to}, device_id_type=mesh_id)
@@ -142,9 +162,9 @@
     ]
     for copy in small:
         copy.start()
-    partners(greet)
     own_series = pltpu.make_async_copy(series, ext.at[pl.ds(8, 512)], series_sem)
     own_series.start()
+    far_first(greet)
     tables = [
         pltpu.make_async_copy(source, target, table_sem.at[n])
         for n, (source, target) in enumerate(
@@ -156,8 +176,6 @@
             )
         )
     ]
-    for copy in tables:
-        copy.start()
 
     for copy in small:
         copy.wait()
@@ -238,7 +256,6 @@
         return body
 
     lax.fori_loop(0, 8, inner(0), 0)
-    lax.fori_loop(1, 7, inner(1), 0)
     pl.semaphore_wait(barrier, SLOTS - 1)
     to_next = pltpu.make_async_remote_copy(
         src_ref=series.at[pl.ds(504, 8)], dst_ref=halos.at[0],
@@ -260,6 +277,9 @@
         to_last.start()
 
     exchange(send1.at[0], recv1.at[0], send1_sem.at[0], recv1_sem.at[0])
+    for copy in tables:
+        copy.start()
+    lax.fori_loop(1, 7, inner(1), 0)
 
     @pl.when(me > 0)
     def _():
@@ -271,10 +291,12 @@
         to_last.wait_recv()
         ext[520:528, :] = halos[1]
 
-    fixes[pl.ds(0, 64, stride=8), :] = jnp.where(lane64 == 0, resample(0, 0), resample(0, 7))
+    def fix(end, held):
+        return jnp.where(lane64 >= 64 * end, resample(0, 7 * end), held)
+
+    fixes[pl.ds(0, 64, stride=8), :] = lax.fori_loop(0, 2, fix, jnp.zeros((64, 128), f32))
     exchange(fixes, fixed, fix_sem.at[0], fix_sem.at[1], 1)
-    for rg in (0, 7):
-        send1[1, pl.ds(rg, 64, stride=8), :] = resample(1, rg)
+    lax.fori_loop(0, 2, lambda end, carry: inner(1)(7 * end, carry), 0)
     exchange(send1.at[1], recv1.at[1], send1_sem.at[1], recv1_sem.at[1])
 
     for copy in tables:

time: 47.4 us -> 45.2 us (0.954)
  Pallas kernels: 45.9 us -> 43.7 us
    pallas_call x1, Pallas kernels: 45.9 us -> 43.7 us  [on_device(): pl.pallas_call(kernel, out_shape=jax.ShapeDtypeStruct((2, 8, 128), f32),...]
where the time goes in v5:
time: 45.2 us; the launch traced here: 45 us
  Pallas kernels  43.7 us (97%)
  local copies, waits for them, and re-layouts  1.3 us (3%)
    pallas_call x1, Pallas kernels, on_device(): pl.pallas_call(kernel, out_shape=jax.ShapeDtypeStruct((2, 8, 128), f32),...  43.7 us
    unnamed x1, local copies, waits for them, and re-layouts  1.3 us

profile of v5, /device:TPU:1, one launch (start us, length us, event | category | flops | bytes accessed | tf_op | source)
XLA Modules:
  0.0 45.0 jit_solution(17251431840715645997)
XLA Ops:
  0.0 43.7 %shard_map.127 = f32[2,8,128]{2,1,0:T(8,128)} custom-call(f32[512,128]{1,0:T(8,128)} %bitcast.3, s32[2,16]{1,0:T(2,128)} %delays.1, s32[2,16]{1,0:T(2,128)} %phases.1, f32[16,32]{1,0:T(8,128)} %bitcast.5, bf16[544,512]{1,0:T(8,128)(2,1)} %constant.18.clone.first_high, bf16[544,512]{1,0:T(8,128)(2,1)} %constant.19.clone.first_low, ...), custom_call_target="tpu_custom_call" | custom-call | tf_op jit(solution)/shard_map/pallas_call | solution.py:525
  43.7 1.3 %copy.16 = f32[2,1,1024]{2,1,0:T(1,128)} copy(f32[2,1,1024]{2,1,0:T(1,128)} %bitcast.4) | data formatting | bytes 16384

commit v6 on v5

--- a/solution.py
+++ b/solution.py
@@ -225,7 +225,7 @@
         both = product(b_high, b_low, w_high, w_low)
         return jnp.where((lane64 & 32) == 0, both[0:64], both[64:128])
 
-    def exchange(source, target, send_sem, recv_sem, rows=8, block_of=lambda device: device):
+    def exchange(source, target, send_sem, recv_sem, rows=8, block_of=lambda device: device, order=partners):
         mine = pl.ds(pl.multiple_of(8 * me, 8), rows)
 
         def block(device):
@@ -238,7 +238,7 @@
                 device_id={"fft": to}, device_id_type=mesh_id,
             ).start()
 
-        partners(send)
+        order(send)
         pltpu.make_async_copy(block(me), target.at[mine], recv_sem).start()
 
     def arrived(target, sem):
@@ -255,7 +255,7 @@
 
         return body
 
-    lax.fori_loop(0, 8, inner(0), 0)
+    lax.fori_loop(0, 8, inner(0), 0, unroll=2)
     pl.semaphore_wait(barrier, SLOTS - 1)
     to_next = pltpu.make_async_remote_copy(
         src_ref=series.at[pl.ds(504, 8)], dst_ref=halos.at[0],
@@ -486,7 +486,7 @@
         transform(trial)
         exchange(
             send2.at[trial], recv2.at[trial], send2_sem.at[trial], recv2_sem.at[trial],
-            block_of=class_at,
+            block_of=class_at, order=far_first if trial else partners,
         )
     for trial in range(2):
         arrived(recv2.at[trial], recv2_sem.at[trial])

time: 45.2 us -> 44.9 us (level)
  no operation moved by 1% of the time
where the time goes in v6:
time: 44.9 us; the launch traced here: 44.8 us
  Pallas kernels  43.5 us (97%)
  local copies, waits for them, and re-layouts  1.3 us (3%)
    pallas_call x1, Pallas kernels, on_device(): pl.pallas_call(kernel, out_shape=jax.ShapeDtypeStruct((2, 8, 128), f32),...  43.5 us
    unnamed x1, local copies, waits for them, and re-layouts  1.3 us

profile of v6, /device:TPU:1, one launch (start us, length us, event | category | flops | bytes accessed | tf_op | source)
XLA Modules:
  0.0 44.8 jit_solution(12239023013893619628)
XLA Ops:
  0.0 43.5 %shard_map.127 = f32[2,8,128]{2,1,0:T(8,128)} custom-call(f32[512,128]{1,0:T(8,128)} %bitcast.3, s32[2,16]{1,0:T(2,128)} %delays.1, s32[2,16]{1,0:T(2,128)} %phases.1, f32[16,32]{1,0:T(8,128)} %bitcast.5, bf16[544,512]{1,0:T(8,128)(2,1)} %constant.18.clone.first_high, bf16[544,512]{1,0:T(8,128)(2,1)} %constant.19.clone.first_low, ...), custom_call_target="tpu_custom_call" | custom-call | tf_op jit(solution)/shard_map/pallas_call | solution.py:525
  43.5 1.3 %copy.16 = f32[2,1,1024]{2,1,0:T(1,128)} copy(f32[2,1,1024]{2,1,0:T(1,128)} %bitcast.4) | data formatting | bytes 16384

commit v7 on v5

--- a/solution.py
+++ b/solution.py
@@ -184,11 +184,10 @@
     second_trial = ((line >> 1) & 1) == 1
     delay = column_of(v_delays[...].astype(f32), own, second_trial)
     phase = column_of(v_phases[...].astype(f32), own, second_trial)
-    branch = (iota((32, PHASES), 1).astype(f32) == phase).astype(f32)
-    taps = lax.dot_general(
-        branch, v_filters[...], (((1,), (1,)), ((), ())),
-        precision=lax.Precision.HIGHEST, preferred_element_type=f32,
-    )
+    taps = jnp.zeros((32, TAPS), f32)
+    filter_rows = v_filters[...].T
+    for number in range(PHASES):
+        taps = jnp.where(phase == float(number), filter_rows[number : number + 1, :], taps)
     position = iota((32, 256), 1).astype(f32) - (delay + 56.0)
     response = jnp.zeros((32, 256), f32)
     for tap in range(TAPS):

time: 45.2 us -> 45.1 us (level)
  no operation moved by 1% of the time
where the time goes in v7:
time: 45.1 us; the launch traced here: 44.9 us
  Pallas kernels  43.6 us (97%)
  local copies, waits for them, and re-layouts  1.3 us (3%)
    pallas_call x1, Pallas kernels, on_device(): pl.pallas_call(kernel, out_shape=jax.ShapeDtypeStruct((2, 8, 128), f32),...  43.6 us
    unnamed x1, local copies, waits for them, and re-layouts  1.3 us

profile of v7, /device:TPU:1, one launch (start us, length us, event | category | flops | bytes accessed | tf_op | source)
XLA Modules:
  0.0 44.9 jit_solution(2404511735059416012)
XLA Ops:
  0.0 43.6 %shard_map.127 = f32[2,8,128]{2,1,0:T(8,128)} custom-call(f32[512,128]{1,0:T(8,128)} %bitcast.3, s32[2,16]{1,0:T(2,128)} %delays.1, s32[2,16]{1,0:T(2,128)} %phases.1, f32[16,32]{1,0:T(8,128)} %bitcast.5, bf16[544,512]{1,0:T(8,128)(2,1)} %constant.18.clone.first_high, bf16[544,512]{1,0:T(8,128)(2,1)} %constant.19.clone.first_low, ...), custom_call_target="tpu_custom_call" | custom-call | tf_op jit(solution)/shard_map/pallas_call | solution.py:524
  43.6 1.3 %copy.16 = f32[2,1,1024]{2,1,0:T(1,128)} copy(f32[2,1,1024]{2,1,0:T(1,128)} %bitcast.4) | data formatting | bytes 16384
